TPU v7x, 32 devices: a whole 2x2x4 slice. The times are simulated.
32 devices in a mesh: dp: 4 (over y, x), fsdp: 8 (over z, core).
Axes of the slice: x: 2, y: 2, z: 4, core: 2. Of those that a mesh axis runs over, the one named last changes fastest.
Arguments:
- tokens: bfloat16 [24576, 1024], P(('dp', 'fsdp')), may hold values from -6 to 6
- segment_ids: int32 [24576], P(('dp', 'fsdp')), may hold values from 0 to 2, as said below
- out_grad: bfloat16 [24576, 1024], P(('dp', 'fsdp')), may hold values from -6 to 6
- norm_gain: bfloat16 [1024], P('fsdp'), may hold values from 0.5 to 1.5
- w_query: bfloat16 [1024, 512], P('fsdp'), may hold values from -0.1875 to 0.1875
- w_key: bfloat16 [1024, 512], P('fsdp'), may hold values from -0.1875 to 0.1875
- w_value: bfloat16 [1024, 1024], P('fsdp'), may hold values from -0.1875 to 0.1875
- w_rank_in: bfloat16 [1024, 16], P('fsdp'), may hold values from -0.1875 to 0.1875
- w_rank_out: bfloat16 [16, 512], P(None, 'fsdp'), may hold values from -0.75 to 0.75
- gate_bias: bfloat16 [512], P('fsdp'), may hold values from 0.3 to 8.5
- w_out_gate: bfloat16 [1024, 1024], P('fsdp'), may hold values from -0.1875 to 0.1875
- head_gain: bfloat16 [256], P('fsdp'), may hold values from 0.5 to 1.5
- w_output: bfloat16 [1024, 1024], P('fsdp'), may hold values from -0.375 to 0.375
- ffn_gain: bfloat16 [1024], P('fsdp'), may hold values from 0.5 to 1.5
- w_gate: bfloat16 [1024, 2816], P('fsdp'), may hold values from -0.1875 to 0.1875
- w_up: bfloat16 [1024, 2816], P('fsdp'), may hold values from -0.1875 to 0.1875
- w_down: bfloat16 [2816, 1024], P('fsdp'), may hold values from -0.21875 to 0.21875
Outputs:
- block_out: bfloat16 [24576, 1024], P(('dp', 'fsdp'))
- input_grad: float32 [24576, 1024], P(('dp', 'fsdp'))
- grad_norm_gain: float32 [1024], P('fsdp')
- grad_query: float32 [1024, 512], P('fsdp')
- grad_key: float32 [1024, 512], P('fsdp')
- grad_value: float32 [1024, 1024], P('fsdp')
- grad_rank_in: float32 [1024, 16], P('fsdp')
- grad_rank_out: float32 [16, 512], P(None, 'fsdp')
- grad_gate_bias: float32 [512], P('fsdp')
- grad_out_gate: float32 [1024, 1024], P('fsdp')
- grad_head_gain: float32 [256], P('fsdp')
- grad_output: float32 [1024, 1024], P('fsdp')
- grad_ffn_gain: float32 [1024], P('fsdp')
- grad_gate: float32 [1024, 2816], P('fsdp')
- grad_up: float32 [1024, 2816], P('fsdp')
- grad_down: float32 [2816, 1024], P('fsdp')
Inputs may be any that keep to these rules, and one draw needn't show every extreme that they name: `segment_ids`: within each micro-batch stream of 3072 tokens the ids do not fall; document 0 ends after at least one token and strictly inside the stream's first 384 tokens, and document 2 begins strictly after the first of the stream's last 384 tokens, so document 1 runs from the first device of fsdp to the last and every change of id lies strictly inside one device's 384 tokens.
All inputs are finite; a program needn't handle non-finite values.
Results may differ from a plain program's by a relative error of at most 0.03.
Values may be sent and summed in bfloat16 or wider, within the bound.
A program may use at most 256 MiB of HBM per device.

v0:
```python
import jax
import jax.numpy as jnp
from jax import lax
from jax.sharding import PartitionSpec as P

HEADS = 4
DK = 128
STRETCH = 64
SLAB = 384


precise = lax.Precision.HIGHEST
eps_norm = 1e-06
eps_head = 0.1


def entering(x, axis, combine, identity):
    count, place = (lax.axis_size(axis), lax.axis_index(axis))
    everything = jax.tree.map(lambda part: lax.all_gather(part, axis), x)
    start = jax.tree.map(
        lambda part, zero: jnp.broadcast_to(jnp.asarray(zero, part.dtype), part.shape), x, identity
    )

    def step(k, before):
        reached = k < place
        new = combine(before, jax.tree.map(lambda part: part[k], everything))
        return jax.tree.map(lambda a, b: jnp.where(reached, a, b), new, before)

    return lax.fori_loop(0, count, step, start)


def entering_2(x, axis, join, neutral):
    count = lax.axis_size(axis)
    place = lax.axis_index(axis)
    ahead = count - 1 - place
    gathered = jax.tree.map(
        lambda a, kind: lax.all_gather(a.astype(kind), axis),
        x,
        jax.tree.map(lambda a: jnp.bfloat16 if a.dtype == jnp.float32 else a.dtype, x),
    )
    state = jax.tree.map(lambda a, e: jnp.zeros_like(a) + jnp.asarray(e, a.dtype), x, neutral)

    def one(step, state):
        source = count - 1 - step
        return join(
            state,
            jax.tree.map(
                lambda a, own: lax.dynamic_index_in_dim(a, source, 0, False).astype(own.dtype),
                gathered,
                x,
            ),
        )

    return lax.fori_loop(0, ahead, one, state)


def half_dot(left, right):
    return jnp.dot(left, right, preferred_element_type=jnp.float32)


def outer_dot(left, right):
    return lax.dot_general(
        left, right, (((0,), (0,)), ((), ())), preferred_element_type=jnp.float32
    )


def trans_dot(left, right):
    return lax.dot_general(
        left, right, (((1,), (1,)), ((), ())), preferred_element_type=jnp.float32
    )


def rounded(values):
    return lax.optimization_barrier(values.astype(jnp.bfloat16)).astype(jnp.float32)


def rms_scale(values, gain):
    return values * lax.rsqrt(jnp.mean(values * values, axis=-1, keepdims=True) + eps_norm) * gain


def head_mix(attended, out_gate, head_gain):
    length = attended.shape[0]
    head_scale = lax.rsqrt(jnp.mean(attended * attended, axis=-1, keepdims=True) + eps_head)
    return (attended * head_scale * head_gain).reshape(length, -1) * jax.nn.silu(out_gate)


def swiglu(gate, upward):
    return jax.nn.silu(gate) * upward


def block_step(carry, block):
    state, previous = carry
    q_block, k_block, v_block, g_block, s_block = block
    cumul = jnp.cumsum(g_block, axis=0)
    width = s_block.shape[0]
    places = jnp.arange(width, dtype=jnp.int32)
    causal = (places[:, None] >= places[None, :]) & (s_block[:, None] == s_block[None, :])
    spread = cumul[:, None] - cumul[None, :]
    spread = jnp.where(causal[:, :, None, None], spread, 0.0)
    factor = jnp.where(causal[:, :, None, None], jnp.exp(spread), 0.0)
    scores = jnp.einsum("ihc,jhc,ijhc->hij", q_block, k_block, factor, precision=precise)
    inner = jnp.einsum("hij,jhv->ihv", scores, v_block, precision=precise)
    keep = (s_block == previous).astype(jnp.float32)
    carried = jnp.einsum(
        "ihc,hcv->ihv", q_block * jnp.exp(cumul) * keep[:, None, None], state, precision=precise
    )
    final_id = s_block[width - 1]
    tail = (
        jnp.exp(cumul[width - 1][None] - cumul)
        * (s_block == final_id).astype(jnp.float32)[:, None, None]
    )
    fresh = jnp.einsum("jhc,jhv->hcv", k_block * tail, v_block, precision=precise)
    new_state = keep[width - 1] * jnp.exp(cumul[width - 1])[:, :, None] * state + fresh
    return ((new_state, final_id), inner + carried)


def gla_core(queries, keys_in, values, log_gate, seg, state_start, prev_start):
    length = queries.shape[0]
    count = length // STRETCH
    blocks = (
        queries.reshape(count, STRETCH, HEADS, -1),
        keys_in.reshape(count, STRETCH, HEADS, -1),
        values.reshape(count, STRETCH, HEADS, -1),
        log_gate.reshape(count, STRETCH, HEADS, -1),
        seg.reshape(count, STRETCH),
    )
    (state, last_id), output = lax.scan(
        jax.checkpoint(block_step), (state_start, prev_start), blocks
    )
    return (output.reshape(length, HEADS, -1), state)


def link_states(earlier, later):
    return (earlier[0] * later[0], later[0][:, :, None] * earlier[1] + later[1])


def chain_forward(coef, local_state):
    scanned = entering(
        (coef, local_state), "fsdp", link_states, (jnp.ones_like(coef), jnp.zeros_like(local_state))
    )
    state_in = scanned[1]
    return state_in


def chain_backward(coef, pulled):
    scanned = entering_2(
        (coef, pulled), "fsdp", link_states, (jnp.ones_like(coef), jnp.zeros_like(pulled))
    )
    state_grad = scanned[1]
    return state_grad


def forward_pass(weights, x_slab, seg_slab):
    (
        norm_gain,
        w_query,
        w_key,
        w_value,
        w_rank_in,
        w_rank_out,
        gate_bias,
        w_out_gate,
        head_gain,
        w_output,
        ffn_gain,
        w_gate,
        w_up,
        w_down,
    ) = weights
    inputs = x_slab.astype(jnp.float32)
    length = inputs.shape[0]
    normed = rms_scale(inputs, norm_gain.astype(jnp.float32)).astype(jnp.bfloat16)
    queries = half_dot(normed, w_query).astype(jnp.bfloat16)
    keys_in = half_dot(normed, w_key).astype(jnp.bfloat16)
    values = half_dot(normed, w_value).astype(jnp.bfloat16)
    rank_mid = half_dot(normed, w_rank_in).astype(jnp.bfloat16)
    gate_pre = half_dot(rank_mid, w_rank_out) + gate_bias.astype(jnp.float32)
    out_gate = half_dot(normed, w_out_gate)
    q_heads = queries.astype(jnp.float32).reshape(length, HEADS, -1) * DK ** (-0.5)
    k_heads = keys_in.astype(jnp.float32).reshape(length, HEADS, -1)
    v_heads = values.astype(jnp.float32).reshape(length, HEADS, -1)
    g_heads = (jax.nn.log_sigmoid(gate_pre) / 16.0).reshape(length, HEADS, -1)
    first_id = seg_slab[0]
    joined = lax.axis_index("fsdp") > 0
    prev_start = jnp.where(joined, first_id, -1)
    keep = ((seg_slab == first_id) & joined).astype(jnp.float32)
    decay = jnp.exp(jnp.cumsum(g_heads, axis=0))
    reach = q_heads * decay * keep[:, None, None]
    coef = keep[length - 1] * decay[length - 1]
    start = jnp.zeros((HEADS, k_heads.shape[2], v_heads.shape[2]), jnp.float32)
    local_out, local_state = gla_core(
        q_heads, k_heads, v_heads, g_heads, seg_slab, start, jnp.array(-1, jnp.int32)
    )
    state_in = chain_forward(coef, local_state)
    attended = local_out + jnp.einsum("thc,hcv->thv", reach, state_in, precision=precise)
    mixed = head_mix(attended, out_gate, head_gain.astype(jnp.float32)).astype(jnp.bfloat16)
    middle = inputs + half_dot(mixed, w_output)
    normed_two = rms_scale(middle, ffn_gain.astype(jnp.float32)).astype(jnp.bfloat16)
    gate = half_dot(normed_two, w_gate)
    upward = half_dot(normed_two, w_up)
    hidden = swiglu(gate, upward).astype(jnp.bfloat16)
    result = middle + half_dot(hidden, w_down)
    saved = (
        inputs,
        normed,
        q_heads,
        k_heads,
        v_heads,
        g_heads,
        rank_mid,
        gate_pre,
        out_gate,
        state_in,
        prev_start,
        reach,
        coef,
        attended,
        mixed,
        middle,
        normed_two,
        gate,
        upward,
        hidden,
    )
    return (saved, result)


def backward_pass(weights, saved, seg_slab, cotangent):
    (
        norm_gain,
        w_query,
        w_key,
        w_value,
        w_rank_in,
        w_rank_out,
        gate_bias,
        w_out_gate,
        head_gain,
        w_output,
        ffn_gain,
        w_gate,
        w_up,
        w_down,
    ) = weights
    (
        inputs,
        normed,
        q_heads,
        k_heads,
        v_heads,
        g_heads,
        rank_mid,
        gate_pre,
        out_gate,
        state_in,
        prev_start,
        reach,
        coef,
        attended,
        mixed,
        middle,
        normed_two,
        gate,
        upward,
        hidden,
    ) = saved
    length = inputs.shape[0]
    d_result = cotangent.astype(jnp.float32)
    d_branch = d_result.astype(jnp.bfloat16)
    g_down = outer_dot(hidden, d_branch)
    d_hidden = rounded(trans_dot(d_branch, w_down))
    unused, pull = jax.vjp(swiglu, gate, upward)
    d_gate, d_up = pull(d_hidden)
    d_gate = d_gate.astype(jnp.bfloat16)
    d_up = d_up.astype(jnp.bfloat16)
    g_gate = outer_dot(normed_two, d_gate)
    g_up = outer_dot(normed_two, d_up)
    d_normed_two = rounded(trans_dot(d_gate, w_gate) + trans_dot(d_up, w_up))
    unused, pull = jax.vjp(rms_scale, middle, ffn_gain.astype(jnp.float32))
    d_middle_part, g_ffn_gain = pull(d_normed_two)
    d_middle = d_result + d_middle_part
    d_attn = d_middle.astype(jnp.bfloat16)
    g_output = outer_dot(mixed, d_attn)
    d_mixed = rounded(trans_dot(d_attn, w_output))
    unused, pull = jax.vjp(head_mix, attended, out_gate, head_gain.astype(jnp.float32))
    d_attended, d_out_gate, g_head_gain = pull(d_mixed)
    pulled = jnp.einsum("thc,thv->hcv", reach, d_attended, precision=precise)
    state_grad = chain_backward(coef, pulled)

    def recurrence(q_in, k_in, v_in, g_in, state_start):
        return gla_core(q_in, k_in, v_in, g_in, seg_slab, state_start, prev_start)

    unused, pull = jax.vjp(recurrence, q_heads, k_heads, v_heads, g_heads, state_in)
    d_q, d_k, d_v, d_g, d_start = pull((d_attended, state_grad))
    d_query = (d_q * DK ** (-0.5)).reshape(length, -1).astype(jnp.bfloat16)
    d_key = d_k.reshape(length, -1).astype(jnp.bfloat16)
    d_value = d_v.reshape(length, -1).astype(jnp.bfloat16)
    d_pre = d_g.reshape(length, -1) / 16.0 * jax.nn.sigmoid(-gate_pre)
    g_bias = jnp.sum(d_pre, axis=0)
    d_pre_low = d_pre.astype(jnp.bfloat16)
    g_rank_out = outer_dot(rank_mid, d_pre_low)
    d_rank = trans_dot(d_pre_low, w_rank_out).astype(jnp.bfloat16)
    g_rank_in = outer_dot(normed, d_rank)
    d_gate_out = d_out_gate.astype(jnp.bfloat16)
    g_out_gate = outer_dot(normed, d_gate_out)
    g_query = outer_dot(normed, d_query)
    g_key = outer_dot(normed, d_key)
    g_value = outer_dot(normed, d_value)
    d_normed = rounded(
        trans_dot(d_query, w_query)
        + trans_dot(d_key, w_key)
        + trans_dot(d_value, w_value)
        + trans_dot(d_rank, w_rank_in)
        + trans_dot(d_gate_out, w_out_gate)
    )
    unused, pull = jax.vjp(rms_scale, inputs, norm_gain.astype(jnp.float32))
    d_input_part, g_norm_gain = pull(d_normed)
    d_input = d_middle + d_input_part
    terms = (
        g_norm_gain,
        g_query,
        g_key,
        g_value,
        g_rank_in,
        g_rank_out,
        g_bias,
        g_out_gate,
        g_head_gain,
        g_output,
        g_ffn_gain,
        g_gate,
        g_up,
        g_down,
    )
    return (terms, d_input)


def on_device(
    tokens,
    segment_ids,
    out_grad,
    norm_gain,
    w_query,
    w_key,
    w_value,
    w_rank_in,
    w_rank_out,
    gate_bias,
    w_out_gate,
    head_gain,
    w_output,
    ffn_gain,
    w_gate,
    w_up,
    w_down,
):
    count = tokens.shape[0] // SLAB
    totals = None
    results = []
    input_grads = []
    for micro_step in range(count):
        row_start = micro_step * SLAB
        x_slab = tokens[row_start : row_start + SLAB]
        seg_slab = segment_ids[row_start : row_start + SLAB]
        cot_slab = out_grad[row_start : row_start + SLAB]
        ahead_weights = (
            lax.all_gather(norm_gain, "fsdp", axis=0, tiled=True),
            lax.all_gather(w_query, "fsdp", axis=0, tiled=True),
            lax.all_gather(w_key, "fsdp", axis=0, tiled=True),
            lax.all_gather(w_value, "fsdp", axis=0, tiled=True),
            lax.all_gather(w_rank_in, "fsdp", axis=0, tiled=True),
            lax.all_gather(w_rank_out, "fsdp", axis=1, tiled=True),
            lax.all_gather(gate_bias, "fsdp", axis=0, tiled=True),
            lax.all_gather(w_out_gate, "fsdp", axis=0, tiled=True),
            lax.all_gather(head_gain, "fsdp", axis=0, tiled=True),
            lax.all_gather(w_output, "fsdp", axis=0, tiled=True),
            lax.all_gather(ffn_gain, "fsdp", axis=0, tiled=True),
            lax.all_gather(w_gate, "fsdp", axis=0, tiled=True),
            lax.all_gather(w_up, "fsdp", axis=0, tiled=True),
            lax.all_gather(w_down, "fsdp", axis=0, tiled=True),
        )
        saved, result = forward_pass(ahead_weights, x_slab, seg_slab)
        behind_weights = (
            lax.all_gather(norm_gain, "fsdp", axis=0, tiled=True),
            lax.all_gather(w_query, "fsdp", axis=0, tiled=True),
            lax.all_gather(w_key, "fsdp", axis=0, tiled=True),
            lax.all_gather(w_value, "fsdp", axis=0, tiled=True),
            lax.all_gather(w_rank_in, "fsdp", axis=0, tiled=True),
            lax.all_gather(w_rank_out, "fsdp", axis=1, tiled=True),
            lax.all_gather(gate_bias, "fsdp", axis=0, tiled=True),
            lax.all_gather(w_out_gate, "fsdp", axis=0, tiled=True),
            lax.all_gather(head_gain, "fsdp", axis=0, tiled=True),
            lax.all_gather(w_output, "fsdp", axis=0, tiled=True),
            lax.all_gather(ffn_gain, "fsdp", axis=0, tiled=True),
            lax.all_gather(w_gate, "fsdp", axis=0, tiled=True),
            lax.all_gather(w_up, "fsdp", axis=0, tiled=True),
            lax.all_gather(w_down, "fsdp", axis=0, tiled=True),
        )
        terms, d_input = backward_pass(behind_weights, saved, seg_slab, cot_slab)
        totals = terms if totals is None else jax.tree.map(jnp.add, totals, terms)
        results.append(result.astype(jnp.bfloat16))
        input_grads.append(d_input)
    (
        t_norm,
        t_query,
        t_key,
        t_value,
        t_rank_in,
        t_rank_out,
        t_bias,
        t_out_gate,
        t_head,
        t_output,
        t_ffn,
        t_gate,
        t_up,
        t_down,
    ) = totals
    owned = (
        lax.psum_scatter(t_norm, "fsdp", scatter_dimension=0, tiled=True),
        lax.psum_scatter(t_query, "fsdp", scatter_dimension=0, tiled=True),
        lax.psum_scatter(t_key, "fsdp", scatter_dimension=0, tiled=True),
        lax.psum_scatter(t_value, "fsdp", scatter_dimension=0, tiled=True),
        lax.psum_scatter(t_rank_in, "fsdp", scatter_dimension=0, tiled=True),
        lax.psum_scatter(t_rank_out, "fsdp", scatter_dimension=1, tiled=True),
        lax.psum_scatter(t_bias, "fsdp", scatter_dimension=0, tiled=True),
        lax.psum_scatter(t_out_gate, "fsdp", scatter_dimension=0, tiled=True),
        lax.psum_scatter(t_head, "fsdp", scatter_dimension=0, tiled=True),
        lax.psum_scatter(t_output, "fsdp", scatter_dimension=0, tiled=True),
        lax.psum_scatter(t_ffn, "fsdp", scatter_dimension=0, tiled=True),
        lax.psum_scatter(t_gate, "fsdp", scatter_dimension=0, tiled=True),
        lax.psum_scatter(t_up, "fsdp", scatter_dimension=0, tiled=True),
        lax.psum_scatter(t_down, "fsdp", scatter_dimension=0, tiled=True),
    )
    (
        o_norm,
        o_query,
        o_key,
        o_value,
        o_rank_in,
        o_rank_out,
        o_bias,
        o_out_gate,
        o_head,
        o_output,
        o_ffn,
        o_gate,
        o_up,
        o_down,
    ) = owned
    summed = (
        lax.psum(o_norm.astype(jnp.bfloat16), "dp").astype(jnp.float32),
        lax.psum(o_query.astype(jnp.bfloat16), "dp").astype(jnp.float32),
        lax.psum(o_key.astype(jnp.bfloat16), "dp").astype(jnp.float32),
        lax.psum(o_value.astype(jnp.bfloat16), "dp").astype(jnp.float32),
        lax.psum(o_rank_in.astype(jnp.bfloat16), "dp").astype(jnp.float32),
        lax.psum(o_rank_out.astype(jnp.bfloat16), "dp").astype(jnp.float32),
        lax.psum(o_bias.astype(jnp.bfloat16), "dp").astype(jnp.float32),
        lax.psum(o_out_gate.astype(jnp.bfloat16), "dp").astype(jnp.float32),
        lax.psum(o_head.astype(jnp.bfloat16), "dp").astype(jnp.float32),
        lax.psum(o_output.astype(jnp.bfloat16), "dp").astype(jnp.float32),
        lax.psum(o_ffn.astype(jnp.bfloat16), "dp").astype(jnp.float32),
        lax.psum(o_gate.astype(jnp.bfloat16), "dp").astype(jnp.float32),
        lax.psum(o_up.astype(jnp.bfloat16), "dp").astype(jnp.float32),
        lax.psum(o_down.astype(jnp.bfloat16), "dp").astype(jnp.float32),
    )
    return (
        jnp.concatenate(results, axis=0),
        jnp.concatenate(input_grads, axis=0),
        summed[0],
        summed[1],
        summed[2],
        summed[3],
        summed[4],
        summed[5],
        summed[6],
        summed[7],
        summed[8],
        summed[9],
        summed[10],
        summed[11],
        summed[12],
        summed[13],
    )


def solution(mesh):
    return jax.shard_map(
        on_device,
        mesh=mesh,
        in_specs=(
            P(("dp", "fsdp"), None),
            P(("dp", "fsdp")),
            P(("dp", "fsdp"), None),
            P("fsdp"),
            P("fsdp", None),
            P("fsdp", None),
            P("fsdp", None),
            P("fsdp", None),
            P(None, "fsdp"),
            P("fsdp"),
            P("fsdp", None),
            P("fsdp"),
            P("fsdp", None),
            P("fsdp"),
            P("fsdp", None),
            P("fsdp", None),
            P("fsdp", None),
        ),
        out_specs=(
            P(("dp", "fsdp"), None),
            P(("dp", "fsdp"), None),
            P("fsdp"),
            P("fsdp", None),
            P("fsdp", None),
            P("fsdp", None),
            P("fsdp", None),
            P(None, "fsdp"),
            P("fsdp"),
            P("fsdp", None),
            P("fsdp"),
            P("fsdp", None),
            P("fsdp"),
            P("fsdp", None),
            P("fsdp", None),
            P("fsdp", None),
        ),
        check_vma=False,
    )
```

profile of v0, /device:TPU:0, one launch (start us, length us, event | category | flops | bytes accessed | tf_op | source)
XLA Modules:
  0.0 1968.8 jit_solution(8355822213385531657)
XLA Ops:
  11.0 14.6 all_gather.53
  25.6 10.7 all-gather.4
  38.0 14.0 all-gather.5
  54.6 13.9 all-reduce.11
  103.0 143.0 %while.170 = (s32[]{:T(128)}, f32[4,128,256]{2,1,0:T(8,128)S(1)}, s32[]{:T(128)}, f32[6,64,4,256]{3,1,0,2:T(8,128)}, s32[6,64]{1,0:T(8,128)S(1)}, /*index=5*/f32...) while((s32[]{:T(128)}, f32[4,128,256]{2,1,0:T(8,128)S(1)}, ...), condition=%wide.region_13.14_spmd.clone, body=%wide.region_11.13_spmd.clone.sunk | while | flops 267055872 | bytes 22436024 | solution.py:127
  104.2 5.9 select_bitcast_fusion.5
  111.2 7.3 fusion.583
  128.1 5.9 select_bitcast_fusion.5
  135.0 7.3 fusion.583
  151.9 5.9 select_bitcast_fusion.5
  158.9 7.3 fusion.583
  175.7 5.9 select_bitcast_fusion.5
  182.6 7.3 fusion.583
  199.5 5.9 select_bitcast_fusion.5
  206.4 7.3 fusion.583
  223.3 5.9 select_bitcast_fusion.5
  230.2 7.3 fusion.583
  257.1 142.7 %while.168 = (s32[]{:T(128)}, f32[4,128,256]{2,1,0:T(8,128)S(1)}, s32[]{:T(128)}, f32[6,64,4,256]{3,1,0,2:T(8,128)}, s32[6,64]{1,0:T(8,128)S(1)}, /*index=5*/f32...) while((s32[]{:T(128)}, f32[4,128,256]{2,1,0:T(8,128)S(1)}, ...), condition=%wide.region_3.4_spmd.clone, body=%wide.region_1.3_spmd.clone.sunk | while | flops 267055872 | bytes 22436024 | solution.py:127
  258.4 5.9 select_bitcast_fusion.4
  265.2 7.4 fusion.570
  282.1 5.9 select_bitcast_fusion.4
  289.0 7.4 fusion.570
  305.9 5.9 select_bitcast_fusion.4
  312.7 7.4 fusion.570
  329.6 5.9 select_bitcast_fusion.4
  336.5 7.4 fusion.570
  353.4 5.9 select_bitcast_fusion.4
  360.2 7.4 fusion.570
  377.1 5.9 select_bitcast_fusion.4
  384.0 7.4 fusion.570
  416.0 13.0 all_gather.59
  435.1 12.7 all_gather.69
  447.8 8.6 all-gather.6
  456.4 10.1 all_gather.145
  466.6 9.7 all_gather.142
  497.3 6.9 convolution_convert_fusion.1
  508.0 10.4 while.171
  518.4 10.5 while.169
  552.2 15.5 all-gather.32.cloned.1.call-done
  567.8 7.3 fusion.295
  575.1 53.3 %all-gather.30.cloned.1.call-done = bf16[1024,2816]{1,0:T(8,128)(2,1)} async-done(((bf16[128,2816]{1,0:T(8,128)(2,1)}), bf16[1024,2816]{1,0:T(8,128)(2,1)}) %all-gather.30.cloned.1.call-update) | async-done | bytes 5767184 | tf_op jit(solution)/shard_map/all_gather | solution.py:378
  628.4 11.0 fusion.152
  658.1 7.3 fusion.155
  701.4 51.2 %while.166 = (s32[]{:T(128)}, f32[4,128,256]{2,1,0:T(8,128)S(1)}, s32[]{:T(128)}, f32[6,4,128,256]{3,2,1,0:T(8,128)}, s32[6]{0:T(128)S(1)}, /*index=5*/s32[6,64]...) while((s32[]{:T(128)}, f32[4,128,256]{2,1,0:T(8,128)S(1)}, ...), condition=%wide.region_42.43_spmd, body=%wide.region_40.42_spmd.sunk | while | flops 103088832 | bytes 3159536 | solution.py:127
  754.7 40.9 %while.163 = (s32[]{:T(128)}, f32[4,128,256]{2,1,0:T(8,128)S(1)}, s32[]{:T(128)}, f32[6,4,128,256]{3,2,1,0:T(8,128)}, s32[6]{0:T(128)S(1)}, /*index=5*/s32[6,64]...) while((s32[]{:T(128)}, f32[4,128,256]{2,1,0:T(8,128)S(1)}, ...), condition=%wide.region_26.27_spmd, body=%wide.region_24.26_spmd.sunk | while | flops 103088832 | bytes 3159536 | solution.py:127
  802.9 8.1 while.165
  813.1 189.7 %while.167 = (s32[]{:T(128)}, f32[4,128,256]{2,1,0:T(8,128)S(1)}, f32[6,64,4,128]{3,2,1,0:T(4,128)S(1)}, bf16[6,64,4,128]{3,2,1,0:T(4,128)(2,1)S(1)}, bf16[6,64,...) while((s32[]{:T(128)}, f32[4,128,256]{2,1,0:T(8,128)S(1)}, ...), condition=%wide.region_50.51_spmd, body=%wide.region_43.50_spmd.sunk | while | flops 565375744 | bytes 15517177 | solution.py:127
  1003.7 12.7 while.162
  1019.5 188.6 %while.164 = (s32[]{:T(128)}, f32[4,128,256]{2,1,0:T(8,128)S(1)}, f32[6,64,4,128]{3,2,1,0:T(4,128)}, bf16[6,64,4,128]{3,2,1,0:T(4,128)(2,1)}, bf16[6,64,4,256]{3...) while((s32[]{:T(128)}, f32[4,128,256]{2,1,0:T(8,128)S(1)}, ...), condition=%wide.region_34.35_spmd, body=%wide.region_27.34_spmd.sunk | while | flops 565375744 | bytes 15516665 | solution.py:127
  1244.8 6.2 convolution_add_fusion.10
  1251.1 6.0 fusion.251
  1257.2 8.7 convolution_add_fusion.9
  1271.4 6.1 convolution_add_fusion.8
  1280.2 6.3 add_convert_fusion.4
  1318.5 17.3 reduce-scatter.21.cloned.1.call-done
  1337.6 48.5 %reduce-scatter.23.cloned.1.call-done = f32[128,1024]{1,0:T(8,128)} async-done(((f32[1024,1024]{1,0:T(8,128)}), f32[128,1024]{1,0:T(8,128)}) %reduce-scatter.23.cloned.1.call-update) | async-done | bytes 524304 | tf_op jit(solution)/shard_map/reduce_scatter | solution.py:429
  1387.9 48.6 %reduce-scatter.17.cloned.1.call-done = f32[128,1024]{1,0:T(8,128)} async-done(((f32[1024,1024]{1,0:T(8,128)}), f32[128,1024]{1,0:T(8,128)}) %reduce-scatter.17.cloned.1.call-update) | async-done | bytes 524304 | tf_op jit(solution)/shard_map/reduce_scatter | solution.py:423
  1438.3 117.9 %reduce-scatter.25.cloned.1.call-done = f32[128,2816]{1,0:T(8,128)} async-done(((f32[1024,2816]{1,0:T(8,128)}), f32[128,2816]{1,0:T(8,128)}) %reduce-scatter.25.cloned.1.call-update) | async-done | bytes 1441808 | tf_op jit(solution)/shard_map/reduce_scatter | solution.py:431
  1558.4 117.7 %reduce-scatter.27.cloned.1.call-done = f32[128,2816]{1,0:T(8,128)} async-done(((f32[1024,2816]{1,0:T(8,128)}), f32[128,2816]{1,0:T(8,128)}) %reduce-scatter.27.cloned.1.call-update) | async-done | bytes 1441808 | tf_op jit(solution)/shard_map/reduce_scatter | solution.py:432
  1678.5 117.6 %reduce-scatter.29.cloned.1.call-done = f32[352,1024]{1,0:T(8,128)} async-done(((f32[2816,1024]{1,0:T(8,128)}), f32[352,1024]{1,0:T(8,128)}) %reduce-scatter.29.cloned.1.call-update) | async-done | bytes 1441808 | tf_op jit(solution)/shard_map/reduce_scatter | solution.py:433
  1811.3 25.9 %all-reduce.10 = (bf16[1024]{0:T(1024)(128)(2,1)S(1)}, bf16[512]{0:T(512)(128)(2,1)S(1)}, bf16[256]{0:T(256)(128)(2,1)S(1)}, bf16[1024]{0:T(1024)(128)(2,1)S(1)}) all-reduce(f32[1024]{0:T(1024)S(1)} %add.483, f32[512]{0:T(512)S(1)} %add.489, f32[256]{0:T(256)S(1)} %copy-done.115, ...), channel_id=6, replica_groups=mesh['dp'=4,'fsdp'=8] {'fsdp'}, use_global_device_ids=true, to_apply=%region_54.55.clone | all-reduce | flops 2816 | bytes 16896
  1842.9 15.2 reduce-scatter.19.cloned.1.call-done
  1858.8 16.2 all-reduce.12
  1878.3 72.9 %all-reduce.16.cloned.1.call-done = (bf16[128,512]{1,0:T(8,128)(2,1)}, bf16[128,512]{1,0:T(8,128)(2,1)}, bf16[128,1024]{1,0:T(8,128)(2,1)}, bf16[128,1024]{1,0:T...) async-done(((bf16[128,512]{1,0:T(8,128)(2,1)}, bf16[128,512]{1,0:T(8,128)(2,1)}, ...) | async-done | bytes 3211280 | tf_op jit(solution)/shard_map/psum | solution.py:453
  (1264 shorter events, 921.4 us)
Async XLA Ops:
  7.2 45.0 %copy-start.116 = (u32[32]{0:T(128)S(1)}, u32[32]{0:T(128)}, u32[]{:S(2)}) copy-start(u32[32]{0:T(128)} %constant.363) | copy-start | bytes 388
  7.2 61.3 %copy-start = (bf16[768,1024]{1,0:T(8,128)(2,1)S(1)}, bf16[768,1024]{1,0:T(8,128)(2,1)}, u32[]{:S(2)}) copy-start(bf16[768,1024]{1,0:T(8,128)(2,1)} %param.37) | copy-start | bytes 4718596
  7.2 30.8 %copy-start.114 = (bf16[16,64]{1,0:T(8,128)(2,1)S(1)}, bf16[16,64]{1,0:T(8,128)(2,1)}, u32[]{:S(2)}) copy-start(bf16[16,64]{1,0:T(8,128)(2,1)} %param.45) | copy-start | bytes 6148
  7.2 46.9 %copy-start.126 = (bf16[64]{0:T(256)(128)(2,1)S(1)}, bf16[64]{0:T(256)(128)(2,1)}, u32[]{:S(2)}) copy-start(bf16[64]{0:T(256)(128)(2,1)} %param.46) | copy-start | bytes 388
  7.2 47.2 %copy-start.127 = (bf16[32]{0:T(256)(128)(2,1)S(1)}, bf16[32]{0:T(256)(128)(2,1)}, u32[]{:S(2)}) copy-start(bf16[32]{0:T(256)(128)(2,1)} %param.48) | copy-start | bytes 196
  7.2 70.8 %all-gather.20.cloned.1.call-start = ((), (), s32[]{:S(2)}) async-start(), calls=%async_computation.10 | async-start | bytes 1179648 | tf_op jit(solution)/shard_map/all_gather | solution.py:369
  8.0 73.1 %all-gather.24.cloned.1.call-start = ((), (), s32[]{:S(2)}) async-start(), calls=%async_computation.12 | async-start | bytes 1179648 | tf_op jit(solution)/shard_map/all_gather | solution.py:368
  8.7 83.4 %all-gather.22.cloned.1.call-start = ((), (), s32[]{:S(2)}) async-start(), calls=%async_computation.11 | async-start | bytes 2359296 | tf_op jit(solution)/shard_map/all_gather | solution.py:370
  9.5 487.9 %all-gather.34.cloned.1.call-start = ((), (), s32[]{:S(2)}) async-start(), calls=%async_computation.17 | async-start | bytes 6488064 | tf_op jit(solution)/shard_map/all_gather | solution.py:380
  10.0 498.0 %all-gather.38.cloned.1.call-start = ((), (), s32[]{:S(2)}) async-start(), calls=%async_computation.28 | async-start | bytes 4718592 | tf_op jit(solution)/shard_map/all_gather | solution.py:19
  25.6 47.8 %copy-start.86 = (bf16[1024,16]{0,1:T(8,128)(2,1)}, bf16[1024,16]{0,1:T(8,128)(2,1)S(1)}, u32[]{:S(2)}) copy-start(bf16[1024,16]{0,1:T(8,128)(2,1)S(1)} %all_gather.53) | copy-start | bytes 98308
  36.2 612.2 %copy-start.78 = (f32[8,1,128]{2,1,0:T(1,128)}, f32[8,1,128]{2,1,0:T(1,128)S(1)}, u32[]{:S(2)}) copy-start(f32[8,1,128]{2,1,0:T(1,128)S(1)} %convert_element_type.568) | copy-start | bytes 12292
  38.0 34.1 %copy-start.106 = (f32[384]{0:T(512)}, f32[384]{0:T(512)S(1)}, u32[]{:S(2)}) copy-start(f32[384]{0:T(512)S(1)} %get-tuple-element.1674) | copy-start | bytes 4612
  38.0 35.3 %copy-start.104 = (f32[384]{0:T(512)}, f32[384]{0:T(512)S(1)}, u32[]{:S(2)}) copy-start(f32[384]{0:T(512)S(1)} %get-tuple-element.1675) | copy-start | bytes 4612
  38.0 504.3 %copy-start.90 = (f32[384]{0:T(512)}, f32[384]{0:T(512)S(1)}, u32[]{:S(2)}) copy-start(f32[384]{0:T(512)S(1)} %fusion.243) | copy-start | bytes 4612
  52.2 21.5 %copy-start.85 = (bf16[512,16]{0,1:T(8,128)(2,1)}, bf16[512,16]{0,1:T(8,128)(2,1)S(1)}, u32[]{:S(2)}) copy-start(bf16[512,16]{0,1:T(8,128)(2,1)S(1)} %reshape.713) | copy-start | bytes 49156
  73.3 575.1 %copy-start.92 = (f32[384]{0:T(512)}, f32[384]{0:T(512)S(1)}, u32[]{:S(2)}) copy-start(f32[384]{0:T(512)S(1)} %fusion.245) | copy-start | bytes 4612
  90.9 5.0 copy-start.62
  255.7 262.7 %all-gather.36.cloned.1.call-start = ((), (), s32[]{:S(2)}) async-start(), calls=%async_computation.27 | async-start | bytes 4718592 | tf_op jit(solution)/shard_map/all_gather | solution.py:19
  400.6 141.8 %all-gather.26.cloned.1.call-start = ((), (), s32[]{:S(2)}) async-start(), calls=%async_computation.13 | async-start | bytes 2359296 | tf_op jit(solution)/shard_map/all_gather | solution.py:374
  401.3 145.7 %all-gather.28.cloned.1.call-start = ((), (), s32[]{:S(2)}) async-start(), calls=%async_computation.14 | async-start | bytes 2359296 | tf_op jit(solution)/shard_map/all_gather | solution.py:376
  402.1 165.7 %all-gather.32.cloned.1.call-start = ((), (), s32[]{:S(2)}) async-start(), calls=%async_computation.16 | async-start | bytes 6488064 | tf_op jit(solution)/shard_map/all_gather | solution.py:379
  402.8 225.6 %all-gather.30.cloned.1.call-start = ((), (), s32[]{:S(2)}) async-start(), calls=%async_computation.15 | async-start | bytes 6488064 | tf_op jit(solution)/shard_map/all_gather | solution.py:378
  403.4 399.5 %all-gather.42.cloned.1.call-start = ((), (), s32[]{:S(2)}) async-start(), calls=%async_computation.30 | async-start | bytes 2359296 | tf_op jit(solution)/shard_map/all_gather | solution.py:37
  414.0 15.0 copy-start.66
  414.3 14.8 copy-start.27
  432.2 15.7 copy-start.117
  497.3 6.9 copy-start.36
  497.3 6.9 copy-start.118
  628.4 11.0 copy-start.120
  643.5 4.9 copy-start.41
  643.5 4.9 copy-start.122
  651.8 19.9 %copy-start.12 = (f32[384,1024]{1,0:T(8,128)}, f32[384,1024]{1,0:T(8,128)S(1)}, u32[]{:S(2)}) copy-start(f32[384,1024]{1,0:T(8,128)S(1)} %get-tuple-element.1957) | copy-start | bytes 4718596
  653.6 4.5 copy-start.19
  689.2 4.5 copy-start.4
  689.2 4.5 copy-start.6
  689.2 4.5 copy-start.8
  699.2 303.7 %all-gather.40.cloned.1.call-start = ((), (), s32[]{:S(2)}) async-start(), calls=%async_computation.29 | async-start | bytes 2359296 | tf_op jit(solution)/shard_map/all_gather | solution.py:37
  802.8 512.5 %reduce-scatter.13.cloned.1.call-start = ((), (), s32[]{:S(2)}) async-start(), calls=%async_computation.18 | async-start | bytes 2359296 | tf_op jit(solution)/shard_map/reduce_scatter | solution.py:421
  1002.8 213.2 %copy-start.34 = (bf16[6,64,4,128]{3,2,1,0:T(4,128)(2,1)}, bf16[6,64,4,128]{3,2,1,0:T(4,128)(2,1)S(1)}, u32[]{:S(2)}) copy-start(bf16[6,64,4,128]{3,2,1,0:T(4,128)(2,1)S(1)} %get-tuple-element.1153) | copy-start | bytes 1179652
  1214.2 102.7 %reduce-scatter.15.cloned.1.call-start = ((), (), s32[]{:S(2)}) async-start(), calls=%async_computation.19 | async-start | bytes 2359296 | tf_op jit(solution)/shard_map/reduce_scatter | solution.py:422
  1218.4 117.5 %reduce-scatter.21.cloned.1.call-start = ((), (), s32[]{:S(2)}) async-start(), calls=%async_computation.22 | async-start | bytes 4718592 | tf_op jit(solution)/shard_map/reduce_scatter | solution.py:427
  1224.2 161.9 %reduce-scatter.23.cloned.1.call-start = ((), (), s32[]{:S(2)}) async-start(), calls=%async_computation.23 | async-start | bytes 4718592 | tf_op jit(solution)/shard_map/reduce_scatter | solution.py:429
  1231.5 205.0 %reduce-scatter.17.cloned.1.call-start = ((), (), s32[]{:S(2)}) async-start(), calls=%async_computation.20 | async-start | bytes 4718592 | tf_op jit(solution)/shard_map/reduce_scatter | solution.py:423
  1239.3 316.8 %reduce-scatter.25.cloned.1.call-start = ((), (), s32[]{:S(2)}) async-start(), calls=%async_computation.24 | async-start | bytes 12976128 | tf_op jit(solution)/shard_map/reduce_scatter | solution.py:431
  1239.6 5.3 copy-start.20
  1239.6 5.3 copy-start.72
  1251.0 425.1 %reduce-scatter.27.cloned.1.call-start = ((), (), s32[]{:S(2)}) async-start(), calls=%async_computation.25 | async-start | bytes 12976128 | tf_op jit(solution)/shard_map/reduce_scatter | solution.py:432
  1251.1 6.1 copy-start.21
  1251.1 6.1 copy-start.70
  1265.9 530.1 %reduce-scatter.29.cloned.1.call-start = ((), (), s32[]{:S(2)}) async-start(), calls=%async_computation.26 | async-start | bytes 12976128 | tf_op jit(solution)/shard_map/reduce_scatter | solution.py:433
  1266.2 5.2 copy-start.38
  1266.2 5.2 copy-start.44
  1277.6 564.6 %reduce-scatter.31.cloned.1.call-start = ((), (), s32[]{:S(2)}) async-start(), calls=%async_computation.31 | async-start | bytes 294912
  1280.2 6.3 copy-start.15
  1280.2 6.3 copy-start.67
  1307.7 550.4 %reduce-scatter.19.cloned.1.call-start = ((), (), s32[]{:S(2)}) async-start(), calls=%async_computation.21 | async-start | bytes 73728 | tf_op jit(solution)/shard_map/reduce_scatter | solution.py:424
  1309.1 642.1 %all-reduce.16.cloned.1.call-start = ((), (), s32[]{:S(2)}) async-start(), calls=%async_computation.32 | async-start | bytes 6422528 | tf_op jit(solution)/shard_map/psum | solution.py:453
  1803.8 6.0 copy-start.25
  1809.8 27.7 %copy-start.107 = (f32[384]{0:T(512)S(1)}, f32[384]{0:T(512)}, u32[]{:S(2)}) copy-start(f32[384]{0:T(512)} %copy-done.106) | copy-start | bytes 4612
  1809.8 27.7 %copy-start.105 = (f32[384]{0:T(512)S(1)}, f32[384]{0:T(512)}, u32[]{:S(2)}) copy-start(f32[384]{0:T(512)} %copy-done.104) | copy-start | bytes 4612
  1951.2 5.2 copy-start.89
  1951.2 6.0 copy-start.88
  1951.2 6.9 copy-start.84
  (88 other events, 176.8 us)
Sparse Core Ops, SparseCore 0:
  9.7 24.8 all-gather.19
  36.2 21.6 all-gather.23
  59.5 28.6 all-gather.21
  89.7 59.9 all-gather.33
  255.8 45.3 all-gather.37
  400.7 45.4 all-gather.35
  447.8 28.0 all-gather.25
  477.5 28.5 all-gather.27
  507.8 59.9 all-gather.31
  569.3 59.0 all-gather.29
  699.3 27.7 all-gather.41
  802.9 27.7 all-gather.39
  1214.3 33.9 reduce-scatter.12
  1250.4 34.5 reduce-scatter.14
  1287.1 48.6 reduce-scatter.20
  1338.0 48.1 reduce-scatter.22
  1388.3 48.1 reduce-scatter.16
  1438.7 117.4 reduce-scatter.24
  1558.5 117.6 reduce-scatter.26
  1678.3 117.6 reduce-scatter.28
  1798.9 28.8 reduce-scatter.30
  1830.0 28.0 reduce-scatter.18
  1863.2 87.9 all-reduce.15
where the time goes:
time: 1990 us; the launch traced here: 1970 us
  waiting for transfers between devices  630 us (32%)
  other arithmetic  595 us (30%)
  matrix products  306 us (15%)
  local copies, waits for them, and re-layouts  236 us (12%)
  blocking collectives  149 us (7%)
  loops' own time  28.3 us (1%)
  between operations  20.7 us (1%)
    while x36, other arithmetic  156 us
    dot_general x24, other arithmetic, block_step(): jnp.einsum('ihc,jhc,ijhc->hij', q_block, k_block, factor, precision=precise)  131 us
    reduce_scatter x1, waiting for transfers between devices, on_device(): lax.psum_scatter(t_gate, 'fsdp', scatter_dimension=0, tiled=True)  118 us
    reduce_scatter x1, waiting for transfers between devices, on_device(): lax.psum_scatter(t_up, 'fsdp', scatter_dimension=0, tiled=True)  118 us
    reduce_scatter x1, waiting for transfers between devices, on_device(): lax.psum_scatter(t_down, 'fsdp', scatter_dimension=0, tiled=True)  118 us
    squeeze x108, local copies, waits for them, and re-layouts, gla_core(): lax.scan(jax.checkpoint(block_step), (state_start, prev_start), blocks)  74.8 us
    psum x1, waiting for transfers between devices, on_device(): lax.psum(o_query.astype(jnp.bfloat16), 'dp').astype(jnp.float32)  72.9 us
    dot_general x20, matrix products, half_dot(): return jnp.dot(left, right, preferred_element_type=jnp.float32)  69.8 us
  transfers between devices with their start and end apart: 23, of which 10 were waited for; matrix products, arithmetic and copies ran while one was open for 42% of the time, Pallas kernels for 0%

commit v1 on v0

v1 whole, which is shorter than its diff:
```python
import functools

import jax
import jax.numpy as jnp
import numpy as np
from jax import lax
from jax.experimental import pallas as pl
from jax.experimental.pallas import tpu as pltpu
from jax.sharding import PartitionSpec as P

HEADS = 4
DK = 128
DV = 256
SLAB = 384
CHUNK = 128
LEVELS = 7
SCALE = DK ** (-0.5)

eps_norm = 1e-06
eps_head = 0.1
bf16 = jnp.bfloat16
f32 = jnp.float32


def nn(left, right):
    return lax.dot_general(
        left.astype(bf16), right.astype(bf16), (((1,), (0,)), ((), ())), preferred_element_type=f32
    )


def tn(left, right):
    return lax.dot_general(
        left.astype(bf16), right.astype(bf16), (((0,), (0,)), ((), ())), preferred_element_type=f32
    )


def nt(left, right):
    return lax.dot_general(
        left.astype(bf16), right.astype(bf16), (((1,), (1,)), ((), ())), preferred_element_type=f32
    )


def rounded(values):
    return lax.optimization_barrier(values.astype(bf16)).astype(f32)


def rms_scale(values, gain):
    return values * lax.rsqrt(jnp.mean(values * values, axis=-1, keepdims=True) + eps_norm) * gain


def head_mix(attended, out_gate, head_gain):
    length = attended.shape[0]
    head_scale = lax.rsqrt(jnp.mean(attended * attended, axis=-1, keepdims=True) + eps_head)
    return (attended * head_scale * head_gain).reshape(length, -1) * jax.nn.silu(out_gate)


def swiglu(gate, upward):
    return jax.nn.silu(gate) * upward


def span_matrix():
    i = np.arange(CHUNK)[:, None]
    s = np.arange(CHUNK)[None, :]
    rows = []
    for level in range(LEVELS):
        half = 1 << level
        mid = (i // (2 * half)) * 2 * half + half - 1
        second = (i >> level) & 1 == 1
        rows.append(np.where(second, (s > mid) & (s <= i), (s > i) & (s <= mid)))
    rows.append(s <= i)
    rows.append(s > i)
    return np.concatenate(rows, axis=0).astype(np.float32)


def part(level):
    return slice(level * CHUNK, (level + 1) * CHUNK)


def chunk_factors(spans, g):
    high = g.astype(bf16)
    low = g - high.astype(f32)
    return jnp.exp(nn(spans, high) + nn(spans, low))


def iotas():
    return (
        lax.broadcasted_iota(jnp.int32, (CHUNK, CHUNK), 0),
        lax.broadcasted_iota(jnp.int32, (CHUNK, CHUNK), 1),
    )


def second_half(level, rows):
    return ((rows >> level) & 1) == 1


def meets(level, rows, columns):
    return ((rows >> (level + 1)) == (columns >> (level + 1))) & (
        (rows >> level) != (columns >> level)
    )


def chunk_scores(q, k, factors, same, rows, columns):
    scores = jnp.where(rows == columns, jnp.sum(q * k, axis=1, keepdims=True), 0.0)
    for level in range(LEVELS):
        mixed = (jnp.where(second_half(level, rows), q, k) * factors[part(level)]).astype(bf16)
        scores = scores + jnp.where(
            meets(level, rows, columns) & (rows > columns), nt(mixed, mixed), 0.0
        )
    return scores * same


def ahead_kernel(
    spans_ref,
    q_ref,
    k_ref,
    v_ref,
    g_ref,
    same_ref,
    keep_ref,
    tail_ref,
    out_ref,
    reach_ref,
    enter_ref,
    enter_coef_ref,
    last_ref,
    coef_ref,
    state,
    decay,
):
    step = pl.program_id(2)

    @pl.when(step == 0)
    def _():
        state[...] = jnp.zeros_like(state)
        decay[...] = jnp.ones_like(decay)

    rows, columns = iotas()
    q = q_ref[...].astype(f32) * SCALE
    k = k_ref[...].astype(f32)
    v = v_ref[...]
    factors = chunk_factors(spans_ref[...], g_ref[...])
    scores = chunk_scores(q, k, factors, same_ref[...].astype(f32), rows, columns)
    carry = factors[part(LEVELS)] * keep_ref[...].astype(f32)
    reach = q * carry
    tail = k * factors[part(LEVELS + 1)] * tail_ref[...].astype(f32)
    before = state[...]
    entering = decay[0:1, :]
    enter_ref[...] = before
    enter_coef_ref[...] = decay[...]
    out_ref[...] = nn(scores, v) + nt(reach, before)
    reach_ref[...] = (reach * entering).astype(bf16)
    coef = carry[CHUNK - 1 : CHUNK, :]
    after = before * coef + tn(v, tail)
    state[...] = after
    decay[...] = decay[...] * coef
    last_ref[...] = after
    coef_ref[...] = decay[...]


def behind_kernel(
    spans_ref,
    q_ref,
    k_ref,
    v_ref,
    g_ref,
    same_ref,
    keep_ref,
    tail_ref,
    enter_ref,
    enter_coef_ref,
    first_ref,
    grad_ref,
    end_ref,
    dq_ref,
    dk_ref,
    dv_ref,
    dg_ref,
    state,
    spread,
):
    step = pl.program_id(2)

    @pl.when(step == 0)
    def _():
        state[...] = end_ref[...]

    rows, columns = iotas()
    q = q_ref[...].astype(f32) * SCALE
    k = k_ref[...].astype(f32)
    v = v_ref[...]
    same = same_ref[...].astype(f32)
    factors = chunk_factors(spans_ref[...], g_ref[...])
    scores = chunk_scores(q, k, factors, same, rows, columns)
    carry = factors[part(LEVELS)] * keep_ref[...].astype(f32)
    reach = q * carry
    leave = factors[part(LEVELS + 1)] * tail_ref[...].astype(f32)
    tail = k * leave
    coef = carry[CHUNK - 1 : CHUNK, :]
    before = enter_ref[...] + enter_coef_ref[0:1, :] * first_ref[...]
    d_out = grad_ref[...].astype(bf16)
    d_after = state[...]

    d_scores = nt(d_out, v) * same
    dv_ref[...] = (tn(scores, d_out) + nt(tail, d_after)).astype(bf16)
    d_reach = nn(d_out, before)
    d_tail = nn(v, d_after)
    d_coef = jnp.sum(d_after * before, axis=0, keepdims=True)
    state[...] = coef * d_after + tn(d_out, reach)

    below = jnp.where(rows > columns, d_scores, 0.0)
    both = below + below.T
    diagonal = jnp.sum(jnp.where(rows == columns, d_scores, 0.0), axis=1, keepdims=True)
    d_q = diagonal * k + d_reach * carry
    d_k = diagonal * q + d_tail * leave
    for level in range(LEVELS):
        second = second_half(level, rows)
        factor = factors[part(level)]
        mixed = jnp.where(second, q, k) * factor
        d_mixed = nn(jnp.where(meets(level, rows, columns), both, 0.0), mixed)
        spread[part(level), :] = (d_mixed * mixed).astype(bf16)
        d_base = d_mixed * factor
        d_q = d_q + jnp.where(second, d_base, 0.0)
        d_k = d_k + jnp.where(second, 0.0, d_base)
    ending = jnp.where(rows == CHUNK - 1, d_coef * coef, 0.0)
    spread[part(LEVELS), :] = (d_reach * reach + ending).astype(bf16)
    spread[part(LEVELS + 1), :] = (d_tail * tail).astype(bf16)
    dg_ref[...] = tn(spans_ref[...], spread[...])
    dq_ref[...] = (d_q * SCALE).astype(bf16)
    dk_ref[...] = d_k.astype(bf16)


def core_specs(chunks, turn):
    def at(m, c):
        return m * chunks + turn(c)

    key = pl.BlockSpec((CHUNK, DK), lambda m, h, c: (at(m, c), h))
    value = pl.BlockSpec((CHUNK, DV), lambda m, h, c: (at(m, c), h))
    plain = pl.BlockSpec((CHUNK, CHUNK), lambda m, h, c: (at(m, c), 0))
    spans = pl.BlockSpec(((LEVELS + 2) * CHUNK, CHUNK), lambda m, h, c: (0, 0))
    enter = pl.BlockSpec((None, None, DV, DK), lambda m, h, c: (at(m, c), h, 0, 0))
    enter_coef = pl.BlockSpec((None, None, 8, DK), lambda m, h, c: (at(m, c), h, 0, 0))
    ends = pl.BlockSpec((None, None, DV, DK), lambda m, h, c: (m, h, 0, 0))
    coef = pl.BlockSpec((None, None, 8, DK), lambda m, h, c: (m, h, 0, 0))
    return key, value, plain, spans, enter, enter_coef, ends, coef


LIMIT = 32 * 1024 * 1024


def core_ahead(spans, q, k, v, g, same, keep, tail):
    total = q.shape[0]
    micro, chunks = total // SLAB, SLAB // CHUNK
    key, value, plain, span, enter, enter_coef, ends, coef = core_specs(chunks, lambda c: c)
    return pl.pallas_call(
        ahead_kernel,
        grid=(micro, HEADS, chunks),
        in_specs=[span, key, key, value, key, plain, plain, plain],
        out_specs=[value, key, enter, enter_coef, ends, coef],
        out_shape=[
            jax.ShapeDtypeStruct((total, HEADS * DV), f32),
            jax.ShapeDtypeStruct((total, HEADS * DK), bf16),
            jax.ShapeDtypeStruct((micro * chunks, HEADS, DV, DK), f32),
            jax.ShapeDtypeStruct((micro * chunks, HEADS, 8, DK), f32),
            jax.ShapeDtypeStruct((micro, HEADS, DV, DK), f32),
            jax.ShapeDtypeStruct((micro, HEADS, 8, DK), f32),
        ],
        scratch_shapes=[pltpu.VMEM((DV, DK), f32), pltpu.VMEM((8, DK), f32)],
        compiler_params=pltpu.CompilerParams(vmem_limit_bytes=LIMIT),
        cost_estimate=pl.CostEstimate(
            flops=12 * total * HEADS * 9 * CHUNK * DK // 2, bytes_accessed=20 * 2**20, transcendentals=0
        ),
        name="core_ahead",
    )(spans, q, k, v, g, same, keep, tail)


def core_behind(spans, q, k, v, g, same, keep, tail, enters, enter_coefs, first, d_out, d_end):
    total = q.shape[0]
    micro, chunks = total // SLAB, SLAB // CHUNK
    key, value, plain, span, enter, enter_coef, ends, coef = core_specs(
        chunks, lambda c: chunks - 1 - c
    )
    return pl.pallas_call(
        behind_kernel,
        grid=(micro, HEADS, chunks),
        in_specs=[span, key, key, value, key, plain, plain, plain]
        + [enter, enter_coef, ends, value, ends],
        out_specs=[key, key, value, key],
        out_shape=[
            jax.ShapeDtypeStruct((total, HEADS * DK), bf16),
            jax.ShapeDtypeStruct((total, HEADS * DK), bf16),
            jax.ShapeDtypeStruct((total, HEADS * DV), bf16),
            jax.ShapeDtypeStruct((total, HEADS * DK), f32),
        ],
        scratch_shapes=[
            pltpu.VMEM((DV, DK), f32),
            pltpu.VMEM(((LEVELS + 2) * CHUNK, DK), bf16),
        ],
        compiler_params=pltpu.CompilerParams(vmem_limit_bytes=LIMIT),
        cost_estimate=pl.CostEstimate(
            flops=24 * total * HEADS * 9 * CHUNK * DK // 2, bytes_accessed=24 * 2**20, transcendentals=0
        ),
        name="core_behind",
    )(spans, q, k, v, g, same, keep, tail, enters, enter_coefs, first, d_out, d_end)


def split_masks(seg, joined):
    micro = seg.shape[0] // SLAB
    chunks = SLAB // CHUNK
    rows = seg.reshape(micro, chunks, CHUNK)
    first = rows[:, 0, 0]
    enter_id = jnp.concatenate(
        [jnp.where(joined, first, -1)[:, None], rows[:, :-1, CHUNK - 1]], axis=1
    )
    keep = rows == enter_id[:, :, None]
    tail = rows == rows[:, :, CHUNK - 1 :]
    same = rows[:, :, :, None] == rows[:, :, None, :]

    def wide(mask):
        return jnp.broadcast_to(mask.astype(bf16).reshape(-1, 1), (seg.shape[0], DK))

    return same.astype(bf16).reshape(-1, CHUNK), wide(keep), wide(tail)


def gathered_rows(x):
    return lax.all_gather(x, "fsdp", axis=0, tiled=True)


def scattered(x):
    return lax.psum_scatter(x.astype(bf16), "fsdp", scatter_dimension=0, tiled=True)


def across(x):
    return lax.psum(x, "dp").astype(f32)


def on_device(
    tokens,
    segment_ids,
    out_grad,
    norm_gain,
    w_query,
    w_key,
    w_value,
    w_rank_in,
    w_rank_out,
    gate_bias,
    w_out_gate,
    head_gain,
    w_output,
    ffn_gain,
    w_gate,
    w_up,
    w_down,
):
    total = tokens.shape[0]
    micro = total // SLAB
    count, place = lax.axis_size("fsdp"), lax.axis_index("fsdp")
    owned_rows = norm_gain.shape[0]
    nq, nv, rank = w_query.shape[1], w_value.shape[1], w_rank_in.shape[1]
    ff = w_gate.shape[1]
    wide_rank = 128
    spans = jnp.asarray(span_matrix(), bf16)

    sizes = [a.size for a in (norm_gain, gate_bias, head_gain, ffn_gain, w_rank_out)]
    cuts = np.cumsum([0] + sizes)
    small = jnp.concatenate(
        [norm_gain, gate_bias, head_gain, ffn_gain, w_rank_out.reshape(-1)]
    )
    small = lax.all_gather(small, "fsdp", axis=0)
    full_norm, full_bias, full_head, full_ffn = (
        small[:, cuts[n] : cuts[n + 1]].reshape(-1) for n in range(4)
    )
    full_rank_out = (
        small[:, cuts[4] : cuts[5]].reshape(count, rank, -1).transpose(1, 0, 2).reshape(rank, -1)
    )
    project = gathered_rows(
        jnp.concatenate(
            [w_query, w_key, w_value, w_out_gate, jnp.pad(w_rank_in, ((0, 0), (0, wide_rank - rank)))],
            axis=1,
        )
    )
    project, w_output, w_gate, w_up, w_down = lax.optimization_barrier(
        (project, w_output, w_gate, w_up, w_down)
    )
    full_output = gathered_rows(w_output)
    full_pair = gathered_rows(jnp.concatenate([w_gate, w_up], axis=1))
    full_down = gathered_rows(w_down)

    inputs = tokens.astype(f32)
    gain_one = full_norm.astype(f32)
    normed = rms_scale(inputs, gain_one).astype(bf16)
    qkv = nn(normed, project[:, : 2 * nq + nv]).astype(bf16)
    queries, keys_in, values = qkv[:, :nq], qkv[:, nq : 2 * nq], qkv[:, 2 * nq :]
    rest = nn(normed, project[:, 2 * nq + nv :])
    out_gate = rest[:, :nv]
    rank_mid = rest[:, nv : nv + rank].astype(bf16)
    gate_pre = nn(rank_mid, full_rank_out) + full_bias.astype(f32)
    log_gate = jax.nn.log_sigmoid(gate_pre) / 16.0

    same, keep, tail = split_masks(segment_ids, place > 0)
    local_out, reach, enters, enter_coefs, local_state, coef = core_ahead(
        spans, queries, keys_in, values, log_gate, same, keep, tail
    )
    coef = coef[:, :, 0, :]
    high = lax.optimization_barrier(coef.astype(bf16))
    low = (coef - high.astype(f32)).astype(bf16)
    lines = micro * HEADS
    parcel = jnp.concatenate(
        [local_state.astype(bf16).reshape(-1, DK), high.reshape(-1, DK), low.reshape(-1, DK)], axis=0
    )
    parcel = lax.all_gather(parcel, "fsdp", axis=0)
    states = parcel[:, : lines * DV].reshape(count, micro, HEADS, DV, DK)
    coefs = (
        parcel[:, lines * DV : lines * (DV + 1)].astype(f32)
        + parcel[:, lines * (DV + 1) :].astype(f32)
    ).reshape(count, micro, HEADS, 1, DK)
    state_in = jnp.zeros((micro, HEADS, DV, DK), f32)
    for k in range(count - 1):
        state_in = jnp.where(k < place, coefs[k] * state_in + states[k].astype(f32), state_in)
    reach_heads = reach.reshape(micro, SLAB, HEADS, DK)
    carried = jnp.einsum(
        "mthc,mhvc->mthv", reach_heads, state_in.astype(bf16), preferred_element_type=f32
    )
    attended = local_out.reshape(total, HEADS, DV) + carried.reshape(total, HEADS, DV)
    gain_head = full_head.astype(f32)
    mixed = head_mix(attended, out_gate, gain_head).astype(bf16)
    middle = inputs + nn(mixed, full_output)
    gain_two = full_ffn.astype(f32)
    normed_two = rms_scale(middle, gain_two).astype(bf16)
    gate = nn(normed_two, full_pair[:, :ff])
    upward = nn(normed_two, full_pair[:, ff:])
    hidden = swiglu(gate, upward).astype(bf16)
    block_out = (middle + nn(hidden, full_down)).astype(bf16)

    d_branch = out_grad
    o_down = scattered(tn(hidden, d_branch))
    d_hidden = rounded(nt(d_branch, full_down))
    _, pull = jax.vjp(swiglu, gate, upward)
    d_pair = jnp.concatenate([a.astype(bf16) for a in pull(d_hidden)], axis=1)
    o_pair = scattered(tn(normed_two, d_pair))
    d_normed_two = rounded(nt(d_pair, full_pair))
    _, pull = jax.vjp(rms_scale, middle, gain_two)
    d_middle_part, g_ffn = pull(d_normed_two)
    d_middle = out_grad.astype(f32) + d_middle_part
    d_attn = d_middle.astype(bf16)
    d_mixed = rounded(nt(d_attn, full_output))
    o_output = scattered(tn(mixed, d_attn))
    _, pull = jax.vjp(head_mix, attended, out_gate, gain_head)
    d_attended, d_out_gate, g_head = pull(d_mixed)
    d_att = d_attended.reshape(total, HEADS * DV)
    pulled = jnp.einsum(
        "mthv,mthc->mhvc",
        d_att.astype(bf16).reshape(micro, SLAB, HEADS, DV),
        reach_heads,
        preferred_element_type=f32,
    )
    pulls = lax.all_gather(pulled.astype(bf16), "fsdp", axis=0)
    d_end = jnp.zeros((micro, HEADS, DV, DK), f32)
    for k in range(count - 1, 0, -1):
        d_end = jnp.where(k > place, coefs[k] * d_end + pulls[k].astype(f32), d_end)
    d_query, d_key, d_value, d_log = core_behind(
        spans, queries, keys_in, values, log_gate, same, keep, tail,
        enters, enter_coefs, state_in, d_att, d_end,
    )
    d_pre = d_log / 16.0 * jax.nn.sigmoid(-gate_pre)
    g_bias = jnp.sum(d_pre, axis=0)
    d_pre_low = d_pre.astype(bf16)
    g_rank_out = tn(rank_mid, d_pre_low)
    d_rank = nt(d_pre_low, full_rank_out).astype(bf16)
    d_project = jnp.concatenate(
        [
            d_query,
            d_key,
            d_value,
            d_out_gate.astype(bf16),
            jnp.pad(d_rank, ((0, 0), (0, wide_rank - rank))),
        ],
        axis=1,
    )
    o_project = scattered(tn(normed, d_project))
    d_normed = rounded(nt(d_project, project))
    _, pull = jax.vjp(rms_scale, inputs, gain_one)
    d_input_part, g_norm = pull(d_normed)
    input_grad = d_middle + d_input_part

    few = jnp.concatenate(
        [
            g_norm.reshape(count, -1),
            g_bias.reshape(count, -1),
            g_head.reshape(count, -1),
            g_ffn.reshape(count, -1),
            g_rank_out.reshape(rank, count, -1).transpose(1, 0, 2).reshape(count, -1),
        ],
        axis=1,
    )
    few = lax.psum(few, ("dp", "fsdp"))
    few = lax.dynamic_index_in_dim(few, place, 0, False)
    s_norm, s_bias, s_head, s_ffn, s_rank_out = (few[cuts[n] : cuts[n + 1]] for n in range(5))
    s_down = across(o_down)
    s_pair = across(o_pair)
    s_output = across(o_output)
    s_project = across(o_project)
    return (
        block_out,
        input_grad,
        s_norm,
        s_project[:, :nq],
        s_project[:, nq : 2 * nq],
        s_project[:, 2 * nq : 2 * nq + nv],
        s_project[:, 2 * nq + 2 * nv : 2 * nq + 2 * nv + rank],
        s_rank_out.reshape(rank, -1),
        s_bias,
        s_project[:, 2 * nq + nv : 2 * nq + 2 * nv],
        s_head,
        s_output,
        s_ffn,
        s_pair[:, :ff],
        s_pair[:, ff:],
        s_down,
    )


def solution(mesh):
    return jax.shard_map(
        on_device,
        mesh=mesh,
        in_specs=(
            P(("dp", "fsdp"), None),
            P(("dp", "fsdp")),
            P(("dp", "fsdp"), None),
            P("fsdp"),
            P("fsdp", None),
            P("fsdp", None),
            P("fsdp", None),
            P("fsdp", None),
            P(None, "fsdp"),
            P("fsdp"),
            P("fsdp", None),
            P("fsdp"),
            P("fsdp", None),
            P("fsdp"),
            P("fsdp", None),
            P("fsdp", None),
            P("fsdp", None),
        ),
        out_specs=(
            P(("dp", "fsdp"), None),
            P(("dp", "fsdp"), None),
            P("fsdp"),
            P("fsdp", None),
            P("fsdp", None),
            P("fsdp", None),
            P("fsdp", None),
            P(None, "fsdp"),
            P("fsdp"),
            P("fsdp", None),
            P("fsdp"),
            P("fsdp", None),
            P("fsdp"),
            P("fsdp", None),
            P("fsdp", None),
            P("fsdp", None),
        ),
        check_vma=False,
    )
```

time: 1990 us -> 893 us (0.45)
  other arithmetic: 595 us -> 43.8 us
  matrix products: 306 us -> 129 us
  local copies, waits for them, and re-layouts: 236 us -> 81.9 us
  waiting for transfers between devices: 630 us -> 485 us
  blocking collectives: 149 us -> 70.2 us
  Pallas kernels: 0 us -> 57.3 us
  loops' own time: 28.3 us -> 0 us
    reduce_scatter x9 -> x4, waiting for transfers between devices: 483 us -> 201 us  [scattered(): lax.psum_scatter(x.astype(bf16), 'fsdp', scatter_dimension=0, tiled=True)]
    all_gather x12 -> x6, waiting for transfers between devices: 68.9 us -> 248 us  [the longest x4 178 us: gathered_rows(): return lax.all_gather(x, 'fsdp', axis=0, tiled=True)]
    dot_general x184 -> x19, matrix products: 306 us -> 129 us  [the longest x7 46.6 us: nn(): lax.dot_general(left.astype(bf16), right.astype(bf16), (((1,), (0,)), (()...]
    while x36 -> x0, other arithmetic: 156 us -> none
    dot_general x24 -> x0, other arithmetic: 131 us -> none  [block_step(): jnp.einsum('ihc,jhc,ijhc->hij', q_block, k_block, factor, precision=precise)]
    all_gather x8 -> x0, blocking collectives: 93.5 us -> none  [the longest x2 25.7 us: entering(): everything = jax.tree.map(lambda part: lax.all_gather(part, axis), x)]
    squeeze x132 -> x0, local copies, waits for them, and re-layouts: 74.8 us -> none  [the longest x108 74.8 us: gla_core(): lax.scan(jax.checkpoint(block_step), (state_start, prev_start), blocks)]
    reduce_sum x37 -> x2, other arithmetic: 61.3 us -> 2.88 us  [the longest x1 2.42 us: head_mix(): jnp.mean(attended * attended, axis=-1, keepdims=True) + eps_head]
  transfers between devices with their start and end apart: 23 -> 11, of which waited for: 10 -> 9; matrix products, arithmetic and copies ran while one was open for 42% -> 15% of each run, Pallas kernels for 0% -> 4%
where the time goes in v1:
time: 893 us; the launch traced here: 883 us
  waiting for transfers between devices  485 us (54%)
  matrix products  129 us (14%)
  local copies, waits for them, and re-layouts  81.9 us (9%)
  blocking collectives  70.2 us (8%)
  Pallas kernels  57.3 us (6%)
  other arithmetic  43.8 us (5%)
  between operations  15.6 us (2%)
    reduce_scatter x4, waiting for transfers between devices, scattered(): lax.psum_scatter(x.astype(bf16), 'fsdp', scatter_dimension=0, tiled=True)  201 us
    all_gather x4, waiting for transfers between devices, gathered_rows(): return lax.all_gather(x, 'fsdp', axis=0, tiled=True)  178 us
    dot_general x7, matrix products, nn(): lax.dot_general(left.astype(bf16), right.astype(bf16), (((1,), (0,)), (()...  46.6 us
    unnamed x153, local copies, waits for them, and re-layouts  44.5 us
    all_gather x1, waiting for transfers between devices, on_device(): parcel = lax.all_gather(parcel, 'fsdp', axis=0)  39.8 us
    dot_general x5, matrix products, tn(): lax.dot_general(left.astype(bf16), right.astype(bf16), (((0,), (0,)), (()...  39.6 us
    psum x1, blocking collectives, on_device(): few = lax.psum(few, ('dp', 'fsdp'))  38.7 us
    dot_general x5, matrix products, nt(): lax.dot_general(left.astype(bf16), right.astype(bf16), (((1,), (1,)), (()...  37.4 us
  transfers between devices with their start and end apart: 11, of which 9 were waited for; matrix products, arithmetic and copies ran while one was open for 15% of the time, Pallas kernels for 4%

profile of v1, /device:TPU:0, one launch (start us, length us, event | category | flops | bytes accessed | tf_op | source)
XLA Modules:
  0.0 883.4 jit_solution(9990536158730021858)
XLA Ops:
  13.7 1.2 dynamic-slice
  15.6 2.8 concatenate.24
  18.7 31.5 %all-reduce.2 = bf16[11008]{0:T(1024)(128)(2,1)S(1)} all-reduce(bf16[11008]{0:T(1024)(128)(2,1)S(1)} %dynamic-update-slice), channel_id=2, replica_groups=mesh['dp'=4,'fsdp'=8] {'fsdp'}, use_global_device_ids=true, to_apply=%add.2 | all-reduce | flops 11008 | bytes 44032
  53.9 29.1 %all-gather.10.cloned.1.call-done = bf16[1024,3200]{1,0:T(8,128)(2,1)} async-done(((bf16[128,3200]{1,0:T(8,128)(2,1)}), bf16[1024,3200]{1,0:T(8,128)(2,1)}) %all-gather.10.cloned.1.call-update) | async-done | bytes 6553616 | tf_op jit(solution)/shard_map/all_gather | solution.py:325
  83.1 4.1 fusion.34
  87.2 3.7 fusion.17
  91.3 2.2 fusion.38
  93.9 23.0 %core_ahead.1 = (f32[768,1024]{1,0:T(8,128)S(1)}, bf16[768,512]{1,0:T(8,128)(2,1)S(1)}, f32[6,4,256,128]{3,2,1,0:T(8,128)S(1)}, f32[6,4,8,128]{3,2,1,0:T(8,128)S...) custom-call(bf16[1152,128]{1,0:T(8,128)(2,1)S(1)} %copy-done.19, ...), custom_call_target="tpu_custom_call" | custom-call | flops 2717908992 | bytes 20971520 | tf_op jit(solution)/shard_map/core_ahead/pallas_call | solution.py:254
  117.0 1.7 copy-done.23
  121.8 2.5 pad_maximum_fusion.5
  124.6 2.4 reshape.316
  127.1 39.8 %all-gather.18.cloned.1.call-done = bf16[16512,128]{1,0:T(8,128)(2,1)} async-done(((bf16[2064,128]{1,0:T(8,128)(2,1)}), bf16[16512,128]{1,0:T(8,128)(2,1)}) %all-gather.18.cloned.1.call-update) | async-done | bytes 4227088 | tf_op jit(solution)/shard_map/all_gather | solution.py:411
  167.6 2.2 fusion.82
  170.9 2.2 convolution_bitcast_fusion
  174.2 3.7 copy.109
  177.8 4.9 copy.108
  182.7 2.4 multiply_reduce_fusion.2
  186.1 2.2 mul.410
  189.1 1.7 copy-done.43
  190.8 2.4 copy.123
  193.5 6.4 multiply_convert_fusion.2
  199.9 4.4 multiply_reduce_fusion.1
  204.4 1.6 copy-done.25
  206.0 1.5 multiply_convert_fusion.1
  207.5 50.2 %all-gather.16.cloned.1.call-done = bf16[2816,1024]{1,0:T(8,128)(2,1)} async-done(((bf16[352,1024]{1,0:T(8,128)(2,1)}), bf16[2816,1024]{1,0:T(8,128)(2,1)}) %all-gather.16.cloned.1.call-update) | async-done | bytes 5767184 | tf_op jit(solution)/shard_map/all_gather | solution.py:325
  257.7 9.8 %fusion.10 = bf16[768,2816]{1,0:T(8,128)(2,1)} fusion(bf16[2816,1024]{1,0:T(8,128)(2,1)} %all-gather.16.cloned.1.call-done, bf16[768,1024]{1,0:T(8,128)(2,1)} %param.20), kind=kOutput, calls=%fused_computation.30 | convolution fusion | flops 4431347712 | bytes 11665408 | tf_op jit(solution)/shard_map/dot_general | solution.py:38
  267.6 99.0 %all-gather.14.cloned.1.call-done = bf16[1024,5632]{1,0:T(8,128)(2,1)} async-done(((bf16[128,5632]{1,0:T(8,128)(2,1)}), bf16[1024,5632]{1,0:T(8,128)(2,1)}) %all-gather.14.cloned.1.call-update) | async-done | bytes 11534352 | tf_op jit(solution)/shard_map/all_gather | solution.py:325
  366.6 8.4 fusion.5
  375.0 13.9 %fusion.3 = (bf16[768,2816]{1,0:T(8,128)(2,1)}, bf16[768,2816]{1,0:T(8,128)(2,1)}, bf16[768,2816]{1,0:T(8,128)(2,1)}) fusion(f32[768,2816]{1,0:T(8,128)S(1)} %fusion.5, bf16[768,2816]{1,0:T(8,128)(2,1)} %fusion.10, bf16[768,1024]{1,0:T(8,128)(2,1)S(1)} %copy-done.53, bf16[1024,5632]{1,0:T(8,128)(2,1)} %all-gather.14.cloned.1.call-done), kind=kOutput, calls=%fused_computation.7 | convolution fusion | flops 4465950720 | bytes 33292288 | tf_op jit(solution)/shard_map/dot_general | solution.py:26
  388.9 16.0 %fusion.36 = bf16[768,1024]{1,0:T(8,128)(2,1)} fusion(bf16[1024,5632]{1,0:T(8,128)(2,1)} %all-gather.14.cloned.1.call-done, bf16[768,2816]{1,0:T(8,128)(2,1)} %get-tuple-element.161, bf16[768,2816]{1,0:T(8,128)(2,1)} %get-tuple-element.159), kind=kOutput, calls=%fused_computation.71 | convolution fusion | flops 8876457984 | bytes 21757952 | tf_op jit(solution)/shard_map/dot_general | solution.py:38
  404.9 3.5 fusion.22
  408.7 2.4 fusion.24
  411.2 1.8 convolution_convert_fusion.6
  413.0 1.6 copy-done.33
  422.9 3.9 fusion.81
  426.7 4.0 reshape.321
  430.7 3.1 fusion.42
  433.9 4.6 convolution_convert_fusion.4
  438.7 10.4 %convolution_convert_fusion.2 = bf16[2816,1024]{1,0:T(8,128)(2,1)} fusion(bf16[768,2816]{1,0:T(8,128)(2,1)} %get-tuple-element.160, bf16[768,1024]{1,0:T(8,128)(2,1)} %param.20), kind=kOutput, calls=%fused_computation.22 | convolution fusion | flops 4432068608 | bytes 11665408 | tf_op jit(solution)/shard_map/dot_general | solution.py:32
  449.2 30.2 %all-gather.20.cloned.1.call-done = bf16[16,4,256,128]{3,2,1,0:T(8,128)(2,1)} async-done(((bf16[2,4,256,128]{3,2,1,0:T(8,128)(2,1)}), bf16[16,4,256,128]{3,2,1,0:T(8,128)(2,1)}) %all-gather.20.cloned.1.call-update) | async-done | bytes 4194320 | tf_op jit(solution)/shard_map/all_gather | solution.py:457
  479.4 3.2 fusion.53.end_ref
  488.7 1.4 copy-done.22
  490.1 1.9 copy-done.24
  492.0 34.3 %core_behind.1 = (bf16[768,512]{1,0:T(8,128)(2,1)S(1)}, bf16[768,512]{1,0:T(8,128)(2,1)S(1)}, bf16[768,1024]{1,0:T(8,128)(2,1)S(1)}, f32[768,512]{1,0:T(8,128)S(1)}) custom-call(bf16[1152,128]{1,0:T(8,128)(2,1)S(1)} %copy-done.20, bf16[768,512]{1,0:T(8,128)(2,1)S(1)} %copy-done.12, bf16[768,512]{1,0:T(8,128)(2,1)S(1)} %copy-done.10, ...), custom_call_target="tpu_custom_call" | custom-call | flops 5435817984 | bytes 25165824 | tf_op jit(solution)/shard_map/core_behind/pallas_call | solution.py:282
  528.8 1.3 constant_dynamic-update-slice_fusion.6
  531.5 3.5 fusion.41
  535.1 2.2 copy-done.58
  537.3 7.9 convolution_convert_fusion.1
  546.6 15.5 %convolution_convert_fusion = bf16[1024,5632]{1,0:T(8,128)(2,1)} fusion(bf16[768,1024]{1,0:T(8,128)(2,1)S(1)} %copy-done.54, bf16[768,2816]{1,0:T(8,128)(2,1)} %get-tuple-element.161, bf16[768,2816]{1,0:T(8,128)(2,1)} %get-tuple-element.159), kind=kOutput, calls=%fused_computation.1 | convolution fusion | flops 8881438720 | bytes 21757952 | tf_op jit(solution)/shard_map/dot_general | solution.py:32
  562.3 1.8 copy-done.27
  564.1 9.8 %add_convert_fusion = bf16[768,1024]{1,0:T(8,128)(2,1)} fusion(f32[768,1024]{1,0:T(8,128)S(1)} %copy-done.27, bf16[768,2816]{1,0:T(8,128)(2,1)} %get-tuple-element.160, bf16[2816,1024]{1,0:T(8,128)(2,1)} %all-gather.16.cloned.1.call-done), kind=kOutput, calls=%fused_computation.60 | convolution fusion | flops 4430757888 | bytes 14811136 | tf_op jit(solution)/shard_map/dot_general | solution.py:26
  573.9 8.2 reduce-scatter.11.cloned.1.call-done
  582.1 73.0 %reduce-scatter.5.cloned.1.call-done = bf16[128,3200]{1,0:T(8,128)(2,1)} async-done(((bf16[1024,3200]{1,0:T(8,128)(2,1)}), bf16[128,3200]{1,0:T(8,128)(2,1)}) %reduce-scatter.5.cloned.1.call-update) | async-done | bytes 819216 | tf_op jit(solution)/shard_map/reduce_scatter | solution.py:329
  655.1 119.9 %reduce-scatter.9.cloned.1.call-done = bf16[128,5632]{1,0:T(8,128)(2,1)} async-done(((bf16[1024,5632]{1,0:T(8,128)(2,1)}), bf16[128,5632]{1,0:T(8,128)(2,1)}) %reduce-scatter.9.cloned.1.call-update) | async-done | bytes 1441808 | tf_op jit(solution)/shard_map/reduce_scatter | solution.py:329
  775.0 9.4 %convolution_convert_fusion.5 = bf16[768,1024]{1,0:T(8,128)(2,1)S(1)} fusion(bf16[768,3200]{1,0:T(8,128)(2,1)} %copy-done.58, bf16[1024,3200]{1,0:T(8,128)(2,1)} %all-gather.10.cloned.1.call-done), kind=kOutput, calls=%fused_computation.72 | convolution fusion | flops 5033951232 | bytes 13041664 | tf_op jit(solution)/shard_map/dot_general | solution.py:38
  784.5 1.2 fusion.66
  786.0 1.4 fusion.23
  787.5 38.7 %psum.35 = f32[8,1376]{1,0:T(8,128)S(1)} all-reduce(f32[8,1376]{1,0:T(8,128)S(1)} %concatenate.31), channel_id=1, replica_groups=mesh['dp'=4,'fsdp'=8] {'dp','fsdp'}, use_global_device_ids=true, to_apply=%region_11.12 | all-reduce | flops 11008 | bytes 88064 | tf_op jit(solution)/shard_map/psum | solution.py:496
  828.7 4.7 fusion.28
  833.4 33.9 %all-reduce.6.cloned.1.call-done = (bf16[128,3200]{1,0:T(8,128)(2,1)}, bf16[128,5632]{1,0:T(8,128)(2,1)}, bf16[128,1024]{1,0:T(8,128)(2,1)}, bf16[352,1024]{1,0:T(8,128)(2,1)}) async-done(((bf16[128,3200]{1,0:T(8,128)(2,1)}, bf16[128,5632]{1,0:T(8,128)(2,1)}, bf16[128,1024]{1,0:T(8,128)(2,1)}, bf16[352,1024]{1,0:T(8,128)(2,1)}), (bf16[128,3200]{1,0:T(8,128)(2,1)}, bf16[128,5632]{1,0:T(8,128)(2,1)}, ...) | async-done | bytes 3244048 | tf_op jit(solution)/shard_map/psum | solution.py:333
  867.3 2.2 fusion.85
  869.5 1.8 fusion.86
  872.1 1.8 fusion.84
  873.9 1.3 convert_element_type.341
  (232 shorter events, 45.1 us)
Async XLA Ops:
  7.2 46.8 %copy-start.65 = (s32[768]{0:T(1024)S(1)}, s32[768]{0:T(1024)}, u32[]{:S(2)}) copy-start(s32[768]{0:T(1024)} %param.19) | copy-start | bytes 9220
  7.2 45.7 %copy-start.38 = (bf16[768,1024]{1,0:T(8,128)(2,1)S(1)}, bf16[768,1024]{1,0:T(8,128)(2,1)}, u32[]{:S(2)}) copy-start(bf16[768,1024]{1,0:T(8,128)(2,1)} %param.18) | copy-start | bytes 4718596
  7.2 75.9 %all-gather.10.cloned.1.call-start = ((), (), s32[]{:S(2)}) async-start(), calls=%async_computation.4 | async-start | bytes 7372800 | tf_op jit(solution)/shard_map/all_gather | solution.py:325
  12.9 153.9 %all-gather.18.cloned.1.call-start = ((), (), s32[]{:S(2)}) async-start(), calls=%async_computation.12 | async-start | bytes 4755456 | tf_op jit(solution)/shard_map/all_gather | solution.py:411
  52.2 41.7 %copy-start.13 = (bf16[768,128]{1,0:T(8,128)(2,1)}, bf16[768,128]{1,0:T(8,128)(2,1)S(1)}, u32[]{:S(2)}) copy-start(bf16[768,128]{1,0:T(8,128)(2,1)S(1)} %fusion.69.same_ref) | copy-start | bytes 589828
  53.9 33.3 %copy-start.61 = (f32[768]{0:T(1024)}, f32[768]{0:T(1024)S(1)}, u32[]{:S(2)}) copy-start(f32[768]{0:T(1024)S(1)} %fusion.71) | copy-start | bytes 9220
  53.9 33.2 %copy-start.59 = (f32[1024]{0:T(1024)}, f32[1024]{0:T(1024)S(1)}, u32[]{:S(2)}) copy-start(f32[1024]{0:T(1024)S(1)} %get-tuple-element.188) | copy-start | bytes 12292
  83.1 4.1 copy-start.66
  87.2 4.1 copy-start.35
  91.1 2.8 copy-start.9
  91.1 2.8 copy-start.11
  91.3 25.7 %copy-start.3 = (bf16[768,1024]{1,0:T(8,128)(2,1)}, bf16[768,1024]{1,0:T(8,128)(2,1)S(1)}, u32[]{:S(2)}) copy-start(bf16[768,1024]{1,0:T(8,128)(2,1)S(1)} %slice.273.v_ref) | copy-start | bytes 4718596
  91.3 2.6 copy-start.19
  93.5 23.4 %copy-start.21 = (f32[768,512]{1,0:T(8,128)}, f32[768,512]{1,0:T(8,128)S(1)}, u32[]{:S(2)}) copy-start(f32[768,512]{1,0:T(8,128)S(1)} %get-tuple-element.191.g_ref) | copy-start | bytes 4718596
  93.7 23.3 %copy-start.15 = (bf16[768,128]{1,0:T(8,128)(2,1)}, bf16[768,128]{1,0:T(8,128)(2,1)S(1)}, u32[]{:S(2)}) copy-start(bf16[768,128]{1,0:T(8,128)(2,1)S(1)} %broadcast_in_dim.17.keep_ref) | copy-start | bytes 589828
  93.9 23.1 %copy-start.17 = (bf16[768,128]{1,0:T(8,128)(2,1)}, bf16[768,128]{1,0:T(8,128)(2,1)S(1)}, u32[]{:S(2)}) copy-start(bf16[768,128]{1,0:T(8,128)(2,1)S(1)} %broadcast_in_dim.18.tail_ref) | copy-start | bytes 589828
  117.0 1.8 copy-start.23
  120.5 79.5 %all-gather.12.cloned.1.call-start = ((), (), s32[]{:S(2)}) async-start(), calls=%async_computation.5 | async-start | bytes 2359296 | tf_op jit(solution)/shard_map/all_gather | solution.py:325
  121.2 136.5 %all-gather.16.cloned.1.call-start = ((), (), s32[]{:S(2)}) async-start(), calls=%async_computation.7 | async-start | bytes 6488064 | tf_op jit(solution)/shard_map/all_gather | solution.py:325
  121.8 244.8 %all-gather.14.cloned.1.call-start = ((), (), s32[]{:S(2)}) async-start(), calls=%async_computation.6 | async-start | bytes 12976128 | tf_op jit(solution)/shard_map/all_gather | solution.py:325
  124.4 355.0 %all-gather.20.cloned.1.call-start = ((), (), s32[]{:S(2)}) async-start(), calls=%async_computation.13 | async-start | bytes 4718592 | tf_op jit(solution)/shard_map/all_gather | solution.py:457
  188.3 2.4 copy-start.43
  189.1 4.1 copy-start.30
  190.8 2.8 copy-start.36
  204.4 1.7 copy-start.25
  366.6 8.4 copy-start.53
  404.9 3.6 copy-start.26
  404.9 3.8 copy-start.47
  408.7 2.4 copy-start.67
  411.1 1.9 copy-start.41
  411.1 3.5 copy-start.33
  411.2 4.6 copy-start.37
  413.0 3.8 copy-start.48
  415.8 1.9 copy-start.32
  416.9 1.8 copy-start.28
  418.8 1.9 copy-start.44
  419.8 2.1 copy-start.29
  419.8 3.0 copy-start.31
  426.7 7.2 copy-start.42
  433.8 140.1 %reduce-scatter.7.cloned.1.call-start = ((), (), s32[]{:S(2)}) async-start(), calls=%async_computation.9 | async-start | bytes 2359296 | tf_op jit(solution)/shard_map/reduce_scatter | solution.py:329
  438.5 143.7 %reduce-scatter.11.cloned.1.call-start = ((), (), s32[]{:S(2)}) async-start(), calls=%async_computation.11 | async-start | bytes 6488064 | tf_op jit(solution)/shard_map/reduce_scatter | solution.py:329
  449.1 33.5 %copy-start.4 = (bf16[768,1024]{1,0:T(8,128)(2,1)S(1)}, bf16[768,1024]{1,0:T(8,128)(2,1)}, u32[]{:S(2)}) copy-start(bf16[768,1024]{1,0:T(8,128)(2,1)} %copy-done.3) | copy-start | bytes 4718596
  449.1 33.5 %copy-start.1 = (f32[2,4,256,128]{3,2,1,0:T(8,128)S(1)}, f32[2,4,256,128]{3,2,1,0:T(8,128)}, u32[]{:S(2)}) copy-start(f32[2,4,256,128]{3,2,1,0:T(8,128)} %copy-done) | copy-start | bytes 3145732
  449.2 206.0 %reduce-scatter.5.cloned.1.call-start = ((), (), s32[]{:S(2)}) async-start(), calls=%async_computation.8 | async-start | bytes 7372800 | tf_op jit(solution)/shard_map/reduce_scatter | solution.py:329
  479.4 3.2 copy-start.2
  490.1 1.9 copy-start.24
  491.9 34.3 %copy-start.52 = (f32[768,512]{1,0:T(8,128)S(1)}, f32[768,512]{1,0:T(8,128)}, u32[]{:S(2)}) copy-start(f32[768,512]{1,0:T(8,128)} %get-tuple-element.192) | copy-start | bytes 4718596
  528.2 1.9 copy-start.6
  528.7 2.3 copy-start.34
  528.7 2.8 copy-start.49
  531.5 5.7 copy-start.39
  531.5 5.7 copy-start.60
  531.5 5.7 copy-start.62
  535.1 2.2 copy-start.58
  545.1 1.4 copy-start.54
  545.2 229.8 %reduce-scatter.9.cloned.1.call-start = ((), (), s32[]{:S(2)}) async-start(), calls=%async_computation.10 | async-start | bytes 12976128 | tf_op jit(solution)/shard_map/reduce_scatter | solution.py:329
  562.1 1.9 copy-start.27
  562.2 305.1 %all-reduce.6.cloned.1.call-start = ((), (), s32[]{:S(2)}) async-start(), calls=%async_computation.14 | async-start | bytes 6488064 | tf_op jit(solution)/shard_map/psum | solution.py:333
  775.0 9.5 %copy-start.46 = (bf16[768,512]{1,0:T(8,128)(2,1)S(1)}, bf16[768,512]{1,0:T(8,128)(2,1)}, u32[]{:S(2)}) copy-start(bf16[768,512]{1,0:T(8,128)(2,1)} %copy-done.45) | copy-start | bytes 2359300
  775.0 11.0 %copy-start.40 = (bf16[768,1024]{1,0:T(8,128)(2,1)S(1)}, bf16[768,1024]{1,0:T(8,128)(2,1)}, u32[]{:S(2)}) copy-start(bf16[768,1024]{1,0:T(8,128)(2,1)} %param.18) | copy-start | bytes 4718596
  784.5 44.2 %copy-start.64 = (f32[768]{0:T(1024)S(1)}, f32[768]{0:T(1024)}, u32[]{:S(2)}) copy-start(f32[768]{0:T(1024)} %copy-done.63) | copy-start | bytes 9220
  867.3 4.9 copy-start.50
  871.3 2.6 copy-start.56
  872.1 3.0 copy-start.57
  (15 other events, 15.3 us)
Sparse Core Ops, SparseCore 0:
  13.0 70.0 all-gather.9
  120.6 46.1 all-gather.17
  168.4 27.8 all-gather.11
  197.8 59.9 all-gather.15
  259.8 106.7 all-gather.13
  433.9 45.4 all-gather.19
  481.7 34.5 reduce-scatter.6
  518.5 63.5 reduce-scatter.10
  584.4 70.6 reduce-scatter.4
  657.3 117.6 reduce-scatter.8
  778.4 88.7 all-reduce.5

commit v2 on v1

--- a/solution.py
+++ b/solution.py
@@ -330,7 +330,40 @@
 
 
 def across(x):
-    return lax.psum(x, "dp").astype(f32)
+    size = lax.axis_size("dp")
+    hop = 1
+    while hop < size:
+        other = lax.ppermute(x, "dp", [(i, i ^ hop) for i in range(size)])
+        whole = x.astype(f32) + other.astype(f32)
+        x = whole.astype(bf16)
+        hop *= 2
+    return whole
+
+
+def pack_state(coef, state):
+    high = lax.optimization_barrier(coef.astype(bf16))
+    low = (coef - high.astype(f32)).astype(bf16)
+    return jnp.concatenate([a.astype(bf16).reshape(-1, DK) for a in (state, high, low)], axis=0)
+
+
+def moved(coef, state, hop):
+    size = lax.axis_size("fsdp")
+    pairs = [(i, i + hop) for i in range(size) if 0 <= i + hop < size]
+    parcel = lax.ppermute(pack_state(coef, state), "fsdp", pairs).astype(f32)
+    lines, rows = coef.size // DK, state.size // DK
+    new_coef = parcel[rows : rows + lines] + parcel[rows + lines :]
+    return new_coef.reshape(coef.shape), parcel[:rows].reshape(state.shape)
+
+
+def entering(coef, state, sign):
+    coef, state = moved(coef, state, sign)
+    hop = 1
+    while hop < lax.axis_size("fsdp"):
+        other_coef, other_state = moved(coef, state, sign * hop)
+        state = coef * other_state + state
+        coef = coef * other_coef
+        hop *= 2
+    return state
 
 
 def on_device(
@@ -366,18 +399,19 @@
     small = jnp.concatenate(
         [norm_gain, gate_bias, head_gain, ffn_gain, w_rank_out.reshape(-1)]
     )
-    small = lax.all_gather(small, "fsdp", axis=0)
+    few_wide = -(-small.shape[0] // owned_rows)
+    small = jnp.pad(small, (0, owned_rows * few_wide - small.shape[0])).reshape(owned_rows, few_wide)
+    base = 2 * nq + 2 * nv
+    blank = jnp.zeros((owned_rows, wide_rank - rank - few_wide), bf16)
+    project = gathered_rows(
+        jnp.concatenate([w_query, w_key, w_value, w_out_gate, w_rank_in, small, blank], axis=1)
+    )
+    small = project[:, base + rank : base + rank + few_wide].reshape(count, -1)
     full_norm, full_bias, full_head, full_ffn = (
         small[:, cuts[n] : cuts[n + 1]].reshape(-1) for n in range(4)
     )
     full_rank_out = (
         small[:, cuts[4] : cuts[5]].reshape(count, rank, -1).transpose(1, 0, 2).reshape(rank, -1)
-    )
-    project = gathered_rows(
-        jnp.concatenate(
-            [w_query, w_key, w_value, w_out_gate, jnp.pad(w_rank_in, ((0, 0), (0, wide_rank - rank)))],
-            axis=1,
-        )
     )
     project, w_output, w_gate, w_up, w_down = lax.optimization_barrier(
         (project, w_output, w_gate, w_up, w_down)
@@ -401,22 +435,8 @@
     local_out, reach, enters, enter_coefs, local_state, coef = core_ahead(
         spans, queries, keys_in, values, log_gate, same, keep, tail
     )
-    coef = coef[:, :, 0, :]
-    high = lax.optimization_barrier(coef.astype(bf16))
-    low = (coef - high.astype(f32)).astype(bf16)
-    lines = micro * HEADS
-    parcel = jnp.concatenate(
-        [local_state.astype(bf16).reshape(-1, DK), high.reshape(-1, DK), low.reshape(-1, DK)], axis=0
-    )
-    parcel = lax.all_gather(parcel, "fsdp", axis=0)
-    states = parcel[:, : lines * DV].reshape(count, micro, HEADS, DV, DK)
-    coefs = (
-        parcel[:, lines * DV : lines * (DV + 1)].astype(f32)
-        + parcel[:, lines * (DV + 1) :].astype(f32)
-    ).reshape(count, micro, HEADS, 1, DK)
-    state_in = jnp.zeros((micro, HEADS, DV, DK), f32)
-    for k in range(count - 1):
-        state_in = jnp.where(k < place, coefs[k] * state_in + states[k].astype(f32), state_in)
+    coef = coef[:, :, 0:1, :]
+    state_in = entering(coef, local_state, 1)
     reach_heads = reach.reshape(micro, SLAB, HEADS, DK)
     carried = jnp.einsum(
         "mthc,mhvc->mthv", reach_heads, state_in.astype(bf16), preferred_element_type=f32
@@ -454,10 +474,7 @@
         reach_heads,
         preferred_element_type=f32,
     )
-    pulls = lax.all_gather(pulled.astype(bf16), "fsdp", axis=0)
-    d_end = jnp.zeros((micro, HEADS, DV, DK), f32)
-    for k in range(count - 1, 0, -1):
-        d_end = jnp.where(k > place, coefs[k] * d_end + pulls[k].astype(f32), d_end)
+    d_end = entering(coef, pulled, -1)
     d_query, d_key, d_value, d_log = core_behind(
         spans, queries, keys_in, values, log_gate, same, keep, tail,
         enters, enter_coefs, state_in, d_att, d_end,
@@ -477,7 +494,7 @@
         ],
         axis=1,
     )
-    o_project = scattered(tn(normed, d_project))
+    g_project = tn(normed, d_project)
     d_normed = rounded(nt(d_project, project))
     _, pull = jax.vjp(rms_scale, inputs, gain_one)
     d_input_part, g_norm = pull(d_normed)
@@ -493,13 +510,19 @@
         ],
         axis=1,
     )
-    few = lax.psum(few, ("dp", "fsdp"))
-    few = lax.dynamic_index_in_dim(few, place, 0, False)
+    few = jnp.pad(few, ((0, 0), (0, owned_rows * few_wide - few.shape[1])))
+    few = few.reshape(count * owned_rows, few_wide)
+    o_project = scattered(
+        jnp.concatenate(
+            [g_project[:, : base + rank], few, g_project[:, base + rank + few_wide :]], axis=1
+        )
+    )
+    s_project = across(o_project)
+    few = s_project[:, base + rank : base + rank + few_wide].reshape(-1)
     s_norm, s_bias, s_head, s_ffn, s_rank_out = (few[cuts[n] : cuts[n + 1]] for n in range(5))
     s_down = across(o_down)
     s_pair = across(o_pair)
     s_output = across(o_output)
-    s_project = across(o_project)
     return (
         block_out,
         input_grad,

time: 893 us -> 834 us (0.934)
  waiting for transfers between devices: 485 us -> 402 us
  starting transfers between devices: 1.06 us -> 76.8 us
  blocking collectives: 70.2 us -> 0 us
    ppermute x0 -> x16, waiting for transfers between devices: none -> 167 us  [the longest x8 113 us: moved(): parcel = lax.ppermute(pack_state(coef, state), 'fsdp', pairs).astype(f32)]
    all_gather x4, waiting for transfers between devices: 178 us -> 94.3 us  [gathered_rows(): return lax.all_gather(x, 'fsdp', axis=0, tiled=True)]
    ppermute x0 -> x16, starting transfers between devices: none -> 76.5 us  [the longest x8 62.7 us: moved(): parcel = lax.ppermute(pack_state(coef, state), 'fsdp', pairs).astype(f32)]
    all_gather x2 -> x0, waiting for transfers between devices: 70 us -> none  [the longest x1 39.8 us: on_device(): parcel = lax.all_gather(parcel, 'fsdp', axis=0)]
    reduce_scatter x4, waiting for transfers between devices: 201 us -> 140 us  [scattered(): lax.psum_scatter(x.astype(bf16), 'fsdp', scatter_dimension=0, tiled=True)]
    psum x1 -> x0, blocking collectives: 38.7 us -> none  [on_device(): few = lax.psum(few, ('dp', 'fsdp'))]
    psum x1 -> x0, waiting for transfers between devices: 33.9 us -> none  [across(): return lax.psum(x, 'dp').astype(f32)]
    unnamed x1 -> x0, blocking collectives: 31.5 us -> none
  transfers between devices with their start and end apart: 11 -> 24, of which waited for: 9 -> 16; matrix products, arithmetic and copies ran while one was open for 15% -> 25% of each run, Pallas kernels for 4% -> 7%
where the time goes in v2:
time: 834 us; the launch traced here: 824 us
  waiting for transfers between devices  402 us (48%)
  matrix products  132 us (16%)
  local copies, waits for them, and re-layouts  90.7 us (11%)
  starting transfers between devices  76.8 us (9%)
  Pallas kernels  57.3 us (7%)
  other arithmetic  49 us (6%)
  between operations  16 us (2%)
    reduce_scatter x4, waiting for transfers between devices, scattered(): lax.psum_scatter(x.astype(bf16), 'fsdp', scatter_dimension=0, tiled=True)  140 us
    ppermute x8, waiting for transfers between devices, moved(): parcel = lax.ppermute(pack_state(coef, state), 'fsdp', pairs).astype(f32)  113 us
    all_gather x4, waiting for transfers between devices, gathered_rows(): return lax.all_gather(x, 'fsdp', axis=0, tiled=True)  94.3 us
    ppermute x8, starting transfers between devices, moved(): parcel = lax.ppermute(pack_state(coef, state), 'fsdp', pairs).astype(f32)  62.7 us
    ppermute x8, waiting for transfers between devices, across(): other = lax.ppermute(x, 'dp', [(i, i ^ hop) for i in range(size)])  54.4 us
    dot_general x7, matrix products, nn(): lax.dot_general(left.astype(bf16), right.astype(bf16), (((1,), (0,)), (()...  50 us
    dot_general x5, matrix products, tn(): lax.dot_general(left.astype(bf16), right.astype(bf16), (((0,), (0,)), (()...  40.2 us
    dot_general x5, matrix products, nt(): lax.dot_general(left.astype(bf16), right.astype(bf16), (((1,), (1,)), (()...  37.2 us
  transfers between devices with their start and end apart: 24, of which 16 were waited for; matrix products, arithmetic and copies ran while one was open for 25% of the time, Pallas kernels for 7%

profile of v2, /device:TPU:0, one launch (start us, length us, event | category | flops | bytes accessed | tf_op | source)
XLA Modules:
  0.0 824.1 jit_solution(15643265743671419812)
XLA Ops:
  8.1 2.8 concatenate.50
  11.9 2.1 concatenate.51
  14.1 69.7 %all-gather.5.cloned.1.call-done = bf16[1024,3200]{1,0:T(8,128)(2,1)} async-done(((bf16[128,3200]{1,0:T(8,128)(2,1)}), bf16[1024,3200]{1,0:T(8,128)(2,1)}) %all-gather.5.cloned.1.call-update) | async-done | bytes 6553616 | tf_op jit(solution)/shard_map/all_gather | solution.py:325
  89.1 6.1 fusion.17
  95.6 4.9 fusion.34
  100.5 2.3 fusion.38
  103.2 23.0 %core_ahead.1 = (f32[768,1024]{1,0:T(8,128)S(1)}, bf16[768,512]{1,0:T(8,128)(2,1)S(1)}, f32[6,4,256,128]{3,2,1,0:T(8,128)S(1)}, f32[6,4,8,128]{3,2,1,0:T(8,128)S...) custom-call(bf16[1152,128]{1,0:T(8,128)(2,1)S(1)} %copy-done.16, ...), custom_call_target="tpu_custom_call" | custom-call | flops 2717908992 | bytes 20971520 | tf_op jit(solution)/shard_map/core_ahead/pallas_call | solution.py:254
  126.5 2.2 collective-permute-start
  130.4 17.9 %collective-permute-start.1 = (bf16[2064,128]{1,0:T(8,128)(2,1)S(1)}, bf16[2064,128]{1,0:T(8,128)(2,1)S(1)}, u32[]{:S(2)}, u32[]{:S(2)}) collective-permute-start(bf16[2064,128]{1,0:T(8,128)(2,1)S(1)} %pad_maximum_fusion.10), channel_id=1, source_target_pairs={{0,1},{1,2},{2,3},{3,4},{4,5},{5,6},{6,7},{8,9},{9,10},{10,11},{11... | collective-permute-start | bytes 1585160 | tf_op jit(solution)/shard_map/ppermute | solution.py:352
  150.9 22.7 %collective-permute-start.2 = (bf16[2064,128]{1,0:T(8,128)(2,1)S(1)}, bf16[2064,128]{1,0:T(8,128)(2,1)S(1)}, u32[]{:S(2)}, u32[]{:S(2)}) collective-permute-start(bf16[2064,128]{1,0:T(8,128)(2,1)S(1)} %pad_maximum_fusion.11), channel_id=1, source_target_pairs={{0,2},{1,3},{2,4},{3,5},{4,6},{5,7},{8,10},{9,11},{10,12},{11,13},... | collective-permute-start | bytes 1585160 | tf_op jit(solution)/shard_map/ppermute | solution.py:352
  173.6 14.6 %collective-permute-done.2 = bf16[2064,128]{1,0:T(8,128)(2,1)S(1)} collective-permute-done((bf16[2064,128]{1,0:T(8,128)(2,1)S(1)}, bf16[2064,128]{1,0:T(8,128)(2,1)S(1)}, u32[]{:S(2)}, u32[]{:S(2)}) %collective-permute-start.2) | collective-permute-done | bytes 528416 | tf_op jit(solution)/shard_map/ppermute | solution.py:352
  190.8 14.8 %collective-permute-start.3 = (bf16[2064,128]{1,0:T(8,128)(2,1)}, bf16[2064,128]{1,0:T(8,128)(2,1)}, u32[]{:S(2)}, u32[]{:S(2)}) collective-permute-start(bf16[2064,128]{1,0:T(8,128)(2,1)} %pad_maximum_fusion.12), channel_id=1, source_target_pairs={{0,4},{1,5},{2,6},{3,7},{8,12},{9,13},{10,14},{11,15},{16,20},{17,... | collective-permute-start | bytes 1585160 | tf_op jit(solution)/shard_map/ppermute | solution.py:352
  207.1 2.4 reshape.561
  212.0 16.0 %collective-permute-done.3 = bf16[2064,128]{1,0:T(8,128)(2,1)} collective-permute-done((bf16[2064,128]{1,0:T(8,128)(2,1)}, bf16[2064,128]{1,0:T(8,128)(2,1)}, u32[]{:S(2)}, u32[]{:S(2)}) %collective-permute-start.3) | collective-permute-done | bytes 528416 | tf_op jit(solution)/shard_map/ppermute | solution.py:352
  229.5 2.2 convolution_bitcast_fusion
  232.7 3.6 copy.110
  236.3 4.9 copy.109
  241.2 4.5 copy.126
  246.8 1.6 copy.112
  248.4 1.9 mul.443
  251.1 1.7 copy-done.29
  253.4 6.4 multiply_convert_fusion.2
  259.8 4.4 multiply_reduce_fusion.1
  267.4 9.9 %fusion.10 = bf16[768,2816]{1,0:T(8,128)(2,1)} fusion(bf16[2816,1024]{1,0:T(8,128)(2,1)} %all-gather.11.cloned.1.call-done, bf16[768,1024]{1,0:T(8,128)(2,1)} %param.20), kind=kOutput, calls=%fused_computation.30 | convolution fusion | flops 4431347712 | bytes 11665408 | tf_op jit(solution)/shard_map/dot_general | solution.py:38
  277.3 24.5 %all-gather.9.cloned.1.call-done = bf16[1024,5632]{1,0:T(8,128)(2,1)} async-done(((bf16[128,5632]{1,0:T(8,128)(2,1)}), bf16[1024,5632]{1,0:T(8,128)(2,1)}) %all-gather.9.cloned.1.call-update) | async-done | bytes 11534352 | tf_op jit(solution)/shard_map/all_gather | solution.py:325
  301.8 8.3 %fusion.5 = f32[768,2816]{1,0:T(8,128)S(1)} fusion(bf16[768,1024]{1,0:T(8,128)(2,1)} %multiply_convert_fusion.1, bf16[1024,5632]{1,0:T(8,128)(2,1)} %all-gather.9.cloned.1.call-done), kind=kOutput, calls=%fused_computation.18 | convolution fusion | flops 4429185024 | bytes 15990784 | tf_op jit(solution)/shard_map/dot_general | solution.py:26
  310.1 14.1 %fusion.3 = (bf16[768,2816]{1,0:T(8,128)(2,1)}, bf16[768,2816]{1,0:T(8,128)(2,1)}, bf16[768,2816]{1,0:T(8,128)(2,1)}) fusion(f32[768,2816]{1,0:T(8,128)S(1)} %fusion.5, bf16[768,2816]{1,0:T(8,128)(2,1)} %fusion.10, bf16[768,1024]{1,0:T(8,128)(2,1)S(1)} %copy-done.59, bf16[1024,5632]{1,0:T(8,128)(2,1)} %all-gather.9.cloned.1.call-done), kind=kOutput, calls=%fused_computation.7 | convolution fusion | flops 4465950720 | bytes 33292288 | tf_op jit(solution)/shard_map/dot_general | solution.py:26
  324.2 8.8 %convolution_convert_fusion.2 = bf16[2816,1024]{1,0:T(8,128)(2,1)} fusion(bf16[768,2816]{1,0:T(8,128)(2,1)} %get-tuple-element.168, bf16[768,1024]{1,0:T(8,128)(2,1)S(1)} %copy-done.57), kind=kOutput, calls=%fused_computation.22 | convolution fusion | flops 4432068608 | bytes 11665408 | tf_op jit(solution)/shard_map/dot_general | solution.py:32
  333.1 15.8 %fusion.36 = bf16[768,1024]{1,0:T(8,128)(2,1)} fusion(bf16[1024,5632]{1,0:T(8,128)(2,1)} %all-gather.9.cloned.1.call-done, bf16[768,2816]{1,0:T(8,128)(2,1)} %get-tuple-element.169, bf16[768,2816]{1,0:T(8,128)(2,1)} %get-tuple-element.167), kind=kOutput, calls=%fused_computation.73 | convolution fusion | flops 8876457984 | bytes 21757952 | tf_op jit(solution)/shard_map/dot_general | solution.py:38
  349.0 4.1 fusion.22
  353.1 2.8 fusion.24
  356.0 1.9 convolution_convert_fusion.6
  367.6 2.9 fusion.77
  370.5 4.0 reshape.566
  374.6 2.3 fusion.42
  378.2 2.5 collective-permute-done.4
  382.2 32.6 %collective-permute-done.5 = bf16[2064,128]{1,0:T(8,128)(2,1)S(1)} collective-permute-done((bf16[2064,128]{1,0:T(8,128)(2,1)S(1)}, bf16[2064,128]{1,0:T(8,128)(2,1)S(1)}, u32[]{:S(2)}, u32[]{:S(2)}) %collective-permute-start.5) | collective-permute-done | bytes 528416 | tf_op jit(solution)/shard_map/ppermute | solution.py:352
  417.2 19.5 %collective-permute-done.6 = bf16[2064,128]{1,0:T(8,128)(2,1)S(1)} collective-permute-done((bf16[2064,128]{1,0:T(8,128)(2,1)S(1)}, bf16[2064,128]{1,0:T(8,128)(2,1)S(1)}, u32[]{:S(2)}, u32[]{:S(2)}) %collective-permute-start.6) | collective-permute-done | bytes 528416 | tf_op jit(solution)/shard_map/ppermute | solution.py:352
  443.2 5.6 convolution_convert_fusion.4
  451.5 24.8 %collective-permute-done.7 = bf16[2064,128]{1,0:T(8,128)(2,1)} collective-permute-done((bf16[2064,128]{1,0:T(8,128)(2,1)}, bf16[2064,128]{1,0:T(8,128)(2,1)}, u32[]{:S(2)}, u32[]{:S(2)}) %collective-permute-start.7) | collective-permute-done | bytes 528416 | tf_op jit(solution)/shard_map/ppermute | solution.py:352
  477.8 34.3 %core_behind.1 = (bf16[768,512]{1,0:T(8,128)(2,1)S(1)}, bf16[768,512]{1,0:T(8,128)(2,1)S(1)}, bf16[768,1024]{1,0:T(8,128)(2,1)S(1)}, f32[768,512]{1,0:T(8,128)S(1)}) custom-call(bf16[1152,128]{1,0:T(8,128)(2,1)S(1)} %copy-done.17, bf16[768,512]{1,0:T(8,128)(2,1)S(1)} %copy-done.13, bf16[768,512]{1,0:T(8,128)(2,1)S(1)} %copy-done.11, ...), custom_call_target="tpu_custom_call" | custom-call | flops 5435817984 | bytes 25165824 | tf_op jit(solution)/shard_map/core_behind/pallas_call | solution.py:282
  518.7 3.3 fusion.41
  522.0 2.2 copy-done.65
  525.5 9.4 %convolution_convert_fusion.5 = bf16[768,1024]{1,0:T(8,128)(2,1)S(1)} fusion(bf16[768,3200]{1,0:T(8,128)(2,1)} %pad_dynamic-update-slice_fusion, bf16[1024,3200]{1,0:T(8,128)(2,1)} %all-gather.5.cloned.1.call-done), kind=kOutput, calls=%fused_computation.74 | convolution fusion | flops 5033951232 | bytes 13041664 | tf_op jit(solution)/shard_map/dot_general | solution.py:38
  538.0 8.4 %convolution_convert_fusion.1 = bf16[1024,3200]{1,0:T(8,128)(2,1)S(1)} fusion(bf16[768,3200]{1,0:T(8,128)(2,1)} %pad_dynamic-update-slice_fusion, bf16[768,1024]{1,0:T(8,128)(2,1)S(1)} %copy-done.39, f32[1024]{0:T(1024)S(1)} %copy-done.74, f32[768]{0:T(1024)S(1)} %copy-done.76), kind=kOutput, calls=%fused_computation.12 | convolution fusion | flops 5039587328 | bytes 13048832 | tf_op jit(solution)/shard_map/dot_general | solution.py:32
  546.4 2.7 copy-done.45
  549.2 11.0 %concatenate.65 = bf16[1024,3200]{1,0:T(8,128)(2,1)} concatenate(bf16[1024,3088]{1,0:T(8,128)(2,1)} %bitcast.167, bf16[1024,11]{1,0:T(8,128)(2,1)S(1)} %reshape.591, bf16[1024,101]{1,0:T(8,128)(2,1)S(1)} %slice.258), dimensions={1} | concatenate | bytes 13107200 | tf_op jit(solution)/shard_map/concatenate | solution.py:516
  561.6 16.1 %convolution_convert_fusion = bf16[1024,5632]{1,0:T(8,128)(2,1)} fusion(bf16[768,1024]{1,0:T(8,128)(2,1)S(1)} %copy-done.60, bf16[768,2816]{1,0:T(8,128)(2,1)} %get-tuple-element.169, bf16[768,2816]{1,0:T(8,128)(2,1)} %get-tuple-element.167), kind=kOutput, calls=%fused_computation.1 | convolution fusion | flops 8881438720 | bytes 21757952 | tf_op jit(solution)/shard_map/dot_general | solution.py:32
  577.8 2.2 collective-permute-start.14
  579.9 9.9 %add_convert_fusion = bf16[768,1024]{1,0:T(8,128)(2,1)} fusion(f32[768,1024]{1,0:T(8,128)S(1)} %copy-done.26, bf16[768,2816]{1,0:T(8,128)(2,1)} %get-tuple-element.168, bf16[2816,1024]{1,0:T(8,128)(2,1)} %all-gather.11.cloned.1.call-done), kind=kOutput, calls=%fused_computation.60 | convolution fusion | flops 4430757888 | bytes 14811136 | tf_op jit(solution)/shard_map/dot_general | solution.py:26
  589.8 1.8 collective-permute-start.10
  591.7 5.6 collective-permute-done.14
  597.2 1.6 add_convert_fusion.3
  598.8 2.1 collective-permute-start.15
  603.5 1.7 collective-permute-start.11
  605.2 26.2 %reduce-scatter.5.cloned.1.call-done = bf16[128,3200]{1,0:T(8,128)(2,1)} async-done(((bf16[1024,3200]{1,0:T(8,128)(2,1)}), bf16[128,3200]{1,0:T(8,128)(2,1)}) %reduce-scatter.5.cloned.1.call-update) | async-done | bytes 819216 | tf_op jit(solution)/shard_map/reduce_scatter | solution.py:329
  632.8 4.9 fusion.28
  637.7 113.7 %reduce-scatter.9.cloned.1.call-done = bf16[128,5632]{1,0:T(8,128)(2,1)} async-done(((bf16[1024,5632]{1,0:T(8,128)(2,1)}), bf16[128,5632]{1,0:T(8,128)(2,1)}) %reduce-scatter.9.cloned.1.call-update) | async-done | bytes 1441808 | tf_op jit(solution)/shard_map/reduce_scatter | solution.py:329
  752.8 1.8 convert_add_fusion.4
  754.6 2.5 convert_add_fusion.3
  758.9 23.9 %collective-permute-done.12 = bf16[128,5632]{1,0:T(8,128)(2,1)S(1)} collective-permute-done((bf16[128,5632]{1,0:T(8,128)(2,1)}, bf16[128,5632]{1,0:T(8,128)(2,1)S(1)}, u32[]{:S(2)}, u32[]{:S(2)}) %collective-permute-start.12) | collective-permute-done | bytes 1441824 | tf_op jit(solution)/shard_map/ppermute | solution.py:336
  790.1 23.4 %collective-permute-done.13 = bf16[128,5632]{1,0:T(8,128)(2,1)} collective-permute-done((bf16[128,5632]{1,0:T(8,128)(2,1)S(1)}, bf16[128,5632]{1,0:T(8,128)(2,1)}, u32[]{:S(2)}, u32[]{:S(2)}) %collective-permute-start.13) | collective-permute-done | bytes 1441824 | tf_op jit(solution)/shard_map/ppermute | solution.py:336
  813.5 1.7 convert_add_fusion.1
  815.2 1.8 fusion.82
  (359 shorter events, 79.1 us)
Async XLA Ops:
  7.2 77.4 %copy-start.63 = (bf16[128,2816]{1,0:T(8,128)(2,1)S(1)}, bf16[128,2816]{1,0:T(8,128)(2,1)}, u32[]{:S(2)}) copy-start(bf16[128,2816]{1,0:T(8,128)(2,1)} %param.33) | copy-start | bytes 2162692
  7.2 77.4 %copy-start.64 = (bf16[128,2816]{1,0:T(8,128)(2,1)S(1)}, bf16[128,2816]{1,0:T(8,128)(2,1)}, u32[]{:S(2)}) copy-start(bf16[128,2816]{1,0:T(8,128)(2,1)} %param.32) | copy-start | bytes 2162692
  7.2 76.6 %all-gather.5.cloned.1.call-start = ((), (), s32[]{:S(2)}) async-start(), calls=%async_computation.4 | async-start | bytes 7372800 | tf_op jit(solution)/shard_map/all_gather | solution.py:325
  14.0 71.9 %copy-start.79 = (s32[768]{0:T(1024)S(1)}, s32[768]{0:T(1024)}, u32[]{:S(2)}) copy-start(s32[768]{0:T(1024)} %param.19) | copy-start | bytes 9220
  14.0 72.8 %copy-start.38 = (bf16[768,1024]{1,0:T(8,128)(2,1)S(1)}, bf16[768,1024]{1,0:T(8,128)(2,1)}, u32[]{:S(2)}) copy-start(bf16[768,1024]{1,0:T(8,128)(2,1)} %param.18) | copy-start | bytes 4718596
  14.0 245.8 %all-gather.7.cloned.1.call-start = ((), (), s32[]{:S(2)}) async-start(), calls=%async_computation.5 | async-start | bytes 2359296 | tf_op jit(solution)/shard_map/all_gather | solution.py:325
  83.8 183.6 %all-gather.11.cloned.1.call-start = ((), (), s32[]{:S(2)}) async-start(), calls=%async_computation.7 | async-start | bytes 6488064 | tf_op jit(solution)/shard_map/all_gather | solution.py:325
  84.6 217.3 %all-gather.9.cloned.1.call-start = ((), (), s32[]{:S(2)}) async-start(), calls=%async_computation.6 | async-start | bytes 12976128 | tf_op jit(solution)/shard_map/all_gather | solution.py:325
  85.8 491.9 %reduce-scatter.11.cloned.1.call-start = ((), (), s32[]{:S(2)}) async-start(), calls=%async_computation.11 | async-start | bytes 6488064 | tf_op jit(solution)/shard_map/reduce_scatter | solution.py:329
  87.2 8.3 %copy-start.75 = (f32[768]{0:T(1024)}, f32[768]{0:T(1024)S(1)}, u32[]{:S(2)}) copy-start(f32[768]{0:T(1024)S(1)} %fusion.64) | copy-start | bytes 9220
  88.6 6.6 copy-start.66
  89.0 11.4 %copy-start.69 = (bf16[16,512]{1,0:T(8,128)(2,1)}, bf16[16,512]{1,0:T(8,128)(2,1)S(1)}, u32[]{:S(2)}) copy-start(bf16[16,512]{1,0:T(8,128)(2,1)S(1)} %reshape.540) | copy-start | bytes 49156
  89.1 6.4 copy-start.73
  95.4 7.7 copy-start.2
  95.6 7.6 copy-start.10
  95.6 7.6 copy-start.12
  102.8 23.4 %copy-start.18 = (f32[768,512]{1,0:T(8,128)}, f32[768,512]{1,0:T(8,128)S(1)}, u32[]{:S(2)}) copy-start(f32[768,512]{1,0:T(8,128)S(1)} %get-tuple-element.184.g_ref) | copy-start | bytes 4718596
  103.1 23.1 %copy-start.14 = (bf16[768,128]{1,0:T(8,128)(2,1)}, bf16[768,128]{1,0:T(8,128)(2,1)S(1)}, u32[]{:S(2)}) copy-start(bf16[768,128]{1,0:T(8,128)(2,1)S(1)} %broadcast_in_dim.20.keep_ref) | copy-start | bytes 589828
  126.4 23.4 %copy-start.82 = (bf16[2,4,1,128]{3,1,2,0:T(4,128)(2,1)}, bf16[2,4,1,128]{3,1,2,0:T(4,128)(2,1)S(1)}, u32[]{:S(2)}) copy-start(bf16[2,4,1,128]{3,1,2,0:T(4,128)(2,1)S(1)} %copy.122) | copy-start | bytes 6148
  126.5 3.7 collective-permute-start
  130.1 18.1 %copy-start.44 = (bf16[2064,128]{1,0:T(8,128)(2,1)}, bf16[2064,128]{1,0:T(8,128)(2,1)S(1)}, u32[]{:S(2)}) copy-start(bf16[2064,128]{1,0:T(8,128)(2,1)S(1)} %collective-permute-done) | copy-start | bytes 1585156
  130.4 19.4 %collective-permute-start.1 = (bf16[2064,128]{1,0:T(8,128)(2,1)S(1)}, bf16[2064,128]{1,0:T(8,128)(2,1)S(1)}, u32[]{:S(2)}, u32[]{:S(2)}) collective-permute-start(bf16[2064,128]{1,0:T(8,128)(2,1)S(1)} %pad_maximum_fusion.10), channel_id=1, source_target_pairs={{0,1},{1,2},{2,3},{3,4},{4,5},{5,6},{6,7},{8,9},{9,10},{10,11},{11... | collective-permute-start | bytes 1585160 | tf_op jit(solution)/shard_map/ppermute | solution.py:352
  150.9 37.3 %collective-permute-start.2 = (bf16[2064,128]{1,0:T(8,128)(2,1)S(1)}, bf16[2064,128]{1,0:T(8,128)(2,1)S(1)}, u32[]{:S(2)}, u32[]{:S(2)}) collective-permute-start(bf16[2064,128]{1,0:T(8,128)(2,1)S(1)} %pad_maximum_fusion.11), channel_id=1, source_target_pairs={{0,2},{1,3},{2,4},{3,5},{4,6},{5,7},{8,10},{9,11},{10,12},{11,13},... | collective-permute-start | bytes 1585160 | tf_op jit(solution)/shard_map/ppermute | solution.py:352
  190.8 37.2 %collective-permute-start.3 = (bf16[2064,128]{1,0:T(8,128)(2,1)}, bf16[2064,128]{1,0:T(8,128)(2,1)}, u32[]{:S(2)}, u32[]{:S(2)}) collective-permute-start(bf16[2064,128]{1,0:T(8,128)(2,1)} %pad_maximum_fusion.12), channel_id=1, source_target_pairs={{0,4},{1,5},{2,6},{3,7},{8,12},{9,13},{10,14},{11,15},{16,20},{17,... | collective-permute-start | bytes 1585160 | tf_op jit(solution)/shard_map/ppermute | solution.py:352
  210.8 18.4 %copy-start.81 = (f32[1,8,128]{2,1,0:T(8,128)S(1)}, f32[1,8,128]{2,1,0:T(8,128)}, u32[]{:S(2)}) copy-start(f32[1,8,128]{2,1,0:T(8,128)} %copy-done.80) | copy-start | bytes 12292
  210.8 18.4 %copy-start.89 = (f32[1,8,128]{2,1,0:T(8,128)S(1)}, f32[1,8,128]{2,1,0:T(8,128)}, u32[]{:S(2)}) copy-start(f32[1,8,128]{2,1,0:T(8,128)} %get-tuple-element.190) | copy-start | bytes 12292
  212.0 17.4 %copy-start.56 = (bf16[2,384,4,128]{3,2,1,0:T(4,128)(2,1)S(1)}, bf16[2,384,4,128]{3,2,1,0:T(4,128)(2,1)}, u32[]{:S(2)}) copy-start(bf16[2,384,4,128]{3,2,1,0:T(4,128)(2,1)} %reshape.561) | copy-start | bytes 2359300
  301.8 8.3 %copy-start.59 = (bf16[768,1024]{1,0:T(8,128)(2,1)S(1)}, bf16[768,1024]{1,0:T(8,128)(2,1)}, u32[]{:S(2)}) copy-start(bf16[768,1024]{1,0:T(8,128)(2,1)} %multiply_convert_fusion.1) | copy-start | bytes 4718596
  310.1 14.2 %copy-start.57 = (bf16[768,1024]{1,0:T(8,128)(2,1)S(1)}, bf16[768,1024]{1,0:T(8,128)(2,1)}, u32[]{:S(2)}) copy-start(bf16[768,1024]{1,0:T(8,128)(2,1)} %param.20) | copy-start | bytes 4718596
  333.1 256.7 %reduce-scatter.7.cloned.1.call-start = ((), (), s32[]{:S(2)}) async-start(), calls=%async_computation.9 | async-start | bytes 2359296 | tf_op jit(solution)/shard_map/reduce_scatter | solution.py:329
  370.5 6.3 copy-start.83
  370.5 6.3 copy-start.85
  376.9 3.8 collective-permute-start.4
  380.9 33.9 %collective-permute-start.5 = (bf16[2064,128]{1,0:T(8,128)(2,1)S(1)}, bf16[2064,128]{1,0:T(8,128)(2,1)S(1)}, u32[]{:S(2)}, u32[]{:S(2)}) collective-permute-start(bf16[2064,128]{1,0:T(8,128)(2,1)S(1)} %pad_maximum_fusion.13), channel_id=1, source_target_pairs={{1,0},{2,1},{3,2},{4,3},{5,4},{6,5},{7,6},{9,8},{10,9},{11,10},{12... | collective-permute-start | bytes 1585160 | tf_op jit(solution)/shard_map/ppermute | solution.py:352
  415.9 20.8 %collective-permute-start.6 = (bf16[2064,128]{1,0:T(8,128)(2,1)S(1)}, bf16[2064,128]{1,0:T(8,128)(2,1)S(1)}, u32[]{:S(2)}, u32[]{:S(2)}) collective-permute-start(bf16[2064,128]{1,0:T(8,128)(2,1)S(1)} %pad_maximum_fusion.14), channel_id=1, source_target_pairs={{2,0},{3,1},{4,2},{5,3},{6,4},{7,5},{10,8},{11,9},{12,10},{13,11},... | collective-permute-start | bytes 1585160 | tf_op jit(solution)/shard_map/ppermute | solution.py:352
  439.3 37.0 %collective-permute-start.7 = (bf16[2064,128]{1,0:T(8,128)(2,1)}, bf16[2064,128]{1,0:T(8,128)(2,1)}, u32[]{:S(2)}, u32[]{:S(2)}) collective-permute-start(bf16[2064,128]{1,0:T(8,128)(2,1)} %pad_maximum_fusion.15), channel_id=1, source_target_pairs={{4,0},{5,1},{6,2},{7,3},{12,8},{13,9},{14,10},{15,11},{20,16},{21,... | collective-permute-start | bytes 1585160 | tf_op jit(solution)/shard_map/ppermute | solution.py:352
  448.8 182.6 %reduce-scatter.5.cloned.1.call-start = ((), (), s32[]{:S(2)}) async-start(), calls=%async_computation.8 | async-start | bytes 7372800 | tf_op jit(solution)/shard_map/reduce_scatter | solution.py:329
  450.0 27.4 %copy-start.88 = (f32[1,8,128]{2,1,0:T(8,128)S(1)}, f32[1,8,128]{2,1,0:T(8,128)}, u32[]{:S(2)}) copy-start(f32[1,8,128]{2,1,0:T(8,128)} %get-tuple-element.192) | copy-start | bytes 12292
  450.0 27.7 %copy-start.21 = (f32[6,4,256,128]{3,2,1,0:T(8,128)S(1)}, f32[6,4,256,128]{3,2,1,0:T(8,128)}, u32[]{:S(2)}) copy-start(f32[6,4,256,128]{3,2,1,0:T(8,128)} %copy-done.20) | copy-start | bytes 9437188
  451.3 26.4 %copy-start.19 = (f32[768,512]{1,0:T(8,128)S(1)}, f32[768,512]{1,0:T(8,128)}, u32[]{:S(2)}) copy-start(f32[768,512]{1,0:T(8,128)} %copy-done.18) | copy-start | bytes 4718596
  451.4 26.3 %copy-start.1 = (f32[2,4,256,128]{3,2,1,0:T(8,128)S(1)}, f32[2,4,256,128]{3,2,1,0:T(8,128)}, u32[]{:S(2)}) copy-start(f32[2,4,256,128]{3,2,1,0:T(8,128)} %copy-done) | copy-start | bytes 3145732
  451.4 26.3 %copy-start.3 = (bf16[768,1024]{1,0:T(8,128)(2,1)S(1)}, bf16[768,1024]{1,0:T(8,128)(2,1)}, u32[]{:S(2)}) copy-start(bf16[768,1024]{1,0:T(8,128)(2,1)} %copy-done.2) | copy-start | bytes 4718596
  451.4 26.3 %copy-start.11 = (bf16[768,512]{1,0:T(8,128)(2,1)S(1)}, bf16[768,512]{1,0:T(8,128)(2,1)}, u32[]{:S(2)}) copy-start(bf16[768,512]{1,0:T(8,128)(2,1)} %copy-done.10) | copy-start | bytes 2359300
  451.4 26.3 %copy-start.13 = (bf16[768,512]{1,0:T(8,128)(2,1)S(1)}, bf16[768,512]{1,0:T(8,128)(2,1)}, u32[]{:S(2)}) copy-start(bf16[768,512]{1,0:T(8,128)(2,1)} %copy-done.12) | copy-start | bytes 2359300
  451.4 26.3 %copy-start.15 = (bf16[768,128]{1,0:T(8,128)(2,1)S(1)}, bf16[768,128]{1,0:T(8,128)(2,1)}, u32[]{:S(2)}) copy-start(bf16[768,128]{1,0:T(8,128)(2,1)} %copy-done.14) | copy-start | bytes 589828
  451.4 26.3 %copy-start.17 = (bf16[1152,128]{1,0:T(8,128)(2,1)S(1)}, bf16[1152,128]{1,0:T(8,128)(2,1)}, u32[]{:S(2)}) copy-start(bf16[1152,128]{1,0:T(8,128)(2,1)} %constant.51.clone.spans_ref) | copy-start | bytes 884740
  451.5 26.3 %copy-start.23 = (f32[6,4,8,128]{3,2,1,0:T(8,128)S(1)}, f32[6,4,8,128]{3,2,1,0:T(8,128)}, u32[]{:S(2)}) copy-start(f32[6,4,8,128]{3,2,1,0:T(8,128)} %copy-done.22) | copy-start | bytes 294916
  477.8 35.5 %copy-start.58 = (f32[768,512]{1,0:T(8,128)S(1)}, f32[768,512]{1,0:T(8,128)}, u32[]{:S(2)}) copy-start(f32[768,512]{1,0:T(8,128)} %get-tuple-element.185) | copy-start | bytes 4718596
  525.5 10.6 %copy-start.39 = (bf16[768,1024]{1,0:T(8,128)(2,1)S(1)}, bf16[768,1024]{1,0:T(8,128)(2,1)}, u32[]{:S(2)}) copy-start(bf16[768,1024]{1,0:T(8,128)(2,1)} %param.18) | copy-start | bytes 4718596
  525.5 10.6 %copy-start.74 = (f32[1024]{0:T(1024)S(1)}, f32[1024]{0:T(1024)}, u32[]{:S(2)}) copy-start(f32[1024]{0:T(1024)} %copy-done.73) | copy-start | bytes 12292
  525.5 10.6 %copy-start.76 = (f32[768]{0:T(1024)S(1)}, f32[768]{0:T(1024)}, u32[]{:S(2)}) copy-start(f32[768]{0:T(1024)} %copy-done.75) | copy-start | bytes 9220
  560.3 191.1 %reduce-scatter.9.cloned.1.call-start = ((), (), s32[]{:S(2)}) async-start(), calls=%async_computation.10 | async-start | bytes 12976128 | tf_op jit(solution)/shard_map/reduce_scatter | solution.py:329
  577.7 12.1 %copy-start.78 = (f32[768]{0:T(1024)S(1)}, f32[768]{0:T(1024)}, u32[]{:S(2)}) copy-start(f32[768]{0:T(1024)} %copy-done.77) | copy-start | bytes 9220
  577.8 19.5 %collective-permute-start.14 = (bf16[352,1024]{1,0:T(8,128)(2,1)}, bf16[352,1024]{1,0:T(8,128)(2,1)}, u32[]{:S(2)}, u32[]{:S(2)}) collective-permute-start(bf16[352,1024]{1,0:T(8,128)(2,1)} %reduce-scatter.11.cloned.1.call-done), channel_id=1, source_target_pairs={{0,8},{8,0},{16,24},{24,16},{1,9},{9,1},{17,25},{25,17},{2,10},{10... | collective-permute-start | bytes 2162696 | tf_op jit(solution)/shard_map/ppermute | solution.py:336
  589.8 43.0 %copy-start.40 = (bf16[768,1024]{1,0:T(8,128)(2,1)S(1)}, bf16[768,1024]{1,0:T(8,128)(2,1)}, u32[]{:S(2)}) copy-start(bf16[768,1024]{1,0:T(8,128)(2,1)} %param.18) | copy-start | bytes 4718596
  589.8 12.7 %collective-permute-start.10 = (bf16[128,1024]{1,0:T(8,128)(2,1)}, bf16[128,1024]{1,0:T(8,128)(2,1)S(1)}, u32[]{:S(2)}, u32[]{:S(2)}) collective-permute-start(bf16[128,1024]{1,0:T(8,128)(2,1)} %reduce-scatter.7.cloned.1.call-done), channel_id=1, source_target_pairs={{0,8},{8,0},{16,24},{24,16},{1,9},{9,1},{17,25},{25,17},{2,10},{10... | collective-permute-start | bytes 786440 | tf_op jit(solution)/shard_map/ppermute | solution.py:336
  598.8 155.8 %collective-permute-start.15 = (bf16[352,1024]{1,0:T(8,128)(2,1)S(1)}, bf16[352,1024]{1,0:T(8,128)(2,1)}, u32[]{:S(2)}, u32[]{:S(2)}) collective-permute-start(bf16[352,1024]{1,0:T(8,128)(2,1)S(1)} %add_convert_fusion.3), channel_id=1, source_target_pairs={{0,16},{8,24},{16,0},{24,8},{1,17},{9,25},{17,1},{25,9},{2,18},{10... | collective-permute-start | bytes 2162696 | tf_op jit(solution)/shard_map/ppermute | solution.py:336
  603.5 149.3 %collective-permute-start.11 = (bf16[128,1024]{1,0:T(8,128)(2,1)S(1)}, bf16[128,1024]{1,0:T(8,128)(2,1)}, u32[]{:S(2)}, u32[]{:S(2)}) collective-permute-start(bf16[128,1024]{1,0:T(8,128)(2,1)S(1)} %add_convert_fusion.4), channel_id=1, source_target_pairs={{0,16},{8,24},{16,0},{24,8},{1,17},{9,25},{17,1},{25,9},{2,18},{10... | collective-permute-start | bytes 786440 | tf_op jit(solution)/shard_map/ppermute | solution.py:336
  631.4 125.8 %collective-permute-start.8 = (bf16[128,3200]{1,0:T(8,128)(2,1)}, bf16[128,3200]{1,0:T(8,128)(2,1)S(1)}, u32[]{:S(2)}, u32[]{:S(2)}) collective-permute-start(bf16[128,3200]{1,0:T(8,128)(2,1)} %reduce-scatter.5.cloned.1.call-done), channel_id=1, source_target_pairs={{0,8},{8,0},{16,24},{24,16},{1,9},{9,1},{17,25},{25,17},{2,10},{10... | collective-permute-start | bytes 2457608 | tf_op jit(solution)/shard_map/ppermute | solution.py:336
  637.7 119.4 %copy-start.62 = (bf16[128,3200]{1,0:T(8,128)(2,1)S(1)}, bf16[128,3200]{1,0:T(8,128)(2,1)}, u32[]{:S(2)}) copy-start(bf16[128,3200]{1,0:T(8,128)(2,1)} %reduce-scatter.5.cloned.1.call-done) | copy-start | bytes 2457604
  751.4 31.4 %copy-start.61 = (bf16[128,5632]{1,0:T(8,128)(2,1)S(1)}, bf16[128,5632]{1,0:T(8,128)(2,1)}, u32[]{:S(2)}) copy-start(bf16[128,5632]{1,0:T(8,128)(2,1)} %reduce-scatter.9.cloned.1.call-done) | copy-start | bytes 4325380
  751.4 31.4 %collective-permute-start.12 = (bf16[128,5632]{1,0:T(8,128)(2,1)}, bf16[128,5632]{1,0:T(8,128)(2,1)S(1)}, u32[]{:S(2)}, u32[]{:S(2)}) collective-permute-start(bf16[128,5632]{1,0:T(8,128)(2,1)} %reduce-scatter.9.cloned.1.call-done), channel_id=1, source_target_pairs={{0,8},{8,0},{16,24},{24,16},{1,9},{9,1},{17,25},{25,17},{2,10},{10... | collective-permute-start | bytes 4325384 | tf_op jit(solution)/shard_map/ppermute | solution.py:336
  757.3 27.3 %collective-permute-start.9 = (bf16[128,3200]{1,0:T(8,128)(2,1)S(1)}, bf16[128,3200]{1,0:T(8,128)(2,1)S(1)}, u32[]{:S(2)}, u32[]{:S(2)}) collective-permute-start(bf16[128,3200]{1,0:T(8,128)(2,1)S(1)} %add_convert_fusion.2), channel_id=1, source_target_pairs={{0,16},{8,24},{16,0},{24,8},{1,17},{9,25},{17,1},{25,9},{2,18},{10... | collective-permute-start | bytes 2457608 | tf_op jit(solution)/shard_map/ppermute | solution.py:336
  783.1 30.4 %collective-permute-start.13 = (bf16[128,5632]{1,0:T(8,128)(2,1)S(1)}, bf16[128,5632]{1,0:T(8,128)(2,1)}, u32[]{:S(2)}, u32[]{:S(2)}) collective-permute-start(bf16[128,5632]{1,0:T(8,128)(2,1)S(1)} %add_convert_fusion.1), channel_id=1, source_target_pairs={{0,16},{8,24},{16,0},{24,8},{1,17},{9,25},{17,1},{25,9},{2,18},{10... | collective-permute-start | bytes 4325384 | tf_op jit(solution)/shard_map/ppermute | solution.py:336
  (54 other events, 131.7 us)
Sparse Core Ops, SparseCore 0:
  14.1 69.6 all-gather.4
  85.4 27.7 all-gather.6
  114.8 68.9 all-gather.10
  185.9 115.8 all-gather.8
  333.2 85.3 reduce-scatter.10
  448.9 43.4 reduce-scatter.6
  560.4 70.9 reduce-scatter.4
  633.7 117.6 reduce-scatter.8
